TPU v7x, 32 devices: a whole 2x2x4 slice. The times are simulated.
32 devices in a mesh: batch: 4 (over z), pencil: 8 (over y, x, core).
Axes of the slice: x: 2, y: 2, z: 4, core: 2. Of those that a mesh axis runs over, the one named last changes fastest.
Arguments:
- state_field: float32 [8, 128, 32, 32, 128], P('batch', 'pencil'), may hold values from -6 to 6
- spectral_weight: float32 [128, 2, 32, 32, 16], P('pencil'), may hold values from -6 to 6
- local_weight: float32 [32, 32], replicated, may hold values from -1 to 1
- channel_bias: float32 [32], replicated, may hold values from -3 to 3
- cotangent: float32 [8, 128, 32, 32, 128], P('batch', 'pencil'), may hold values from -6 to 6
Outputs:
- layer_out: float32 [8, 128, 32, 32, 128], P('batch', 'pencil')
- grad_state: float32 [8, 128, 32, 32, 128], P('batch', 'pencil')
- grad_spectral: float32 [128, 2, 32, 32, 16], P('pencil')
- grad_local: float32 [32, 32], replicated
- grad_bias: float32 [32], replicated
All inputs are finite; a program needn't handle non-finite values.
Results may differ from a plain program's by a relative error of at most 0.00011.
Values sent between devices are 32-bit elements; how exact they have to be, the bound alone decides.
No kernel may reach another device: no remote copies, remote signals or barrier semaphores. Data moves between devices by JAX's collectives and lax.ppermute only.
A program may use at most 256 MiB of HBM per device.

v0:
```python
import math

import jax
import jax.numpy as jnp
from jax import lax
from jax.sharding import PartitionSpec as P

X = 128
Y = 128
Z = 32
MX = 16
MY = 16
MZ = 8


gelu_scale = math.sqrt(2.0 / math.pi)
cubic_term = 0.044715


def contract(form, left, right):
    return jnp.einsum(form, left, right, precision=lax.Precision.HIGHEST)


def tables(points, kept_modes):
    position = jnp.arange(points, dtype=jnp.int32)
    mode_order = jnp.arange(kept_modes, dtype=jnp.int32)
    frequency = jnp.where(
        mode_order < kept_modes // 2, mode_order, points - kept_modes + mode_order
    )
    phases = position[:, None] * frequency[None, :] % points
    angles = phases.astype(jnp.float32) * (2.0 * math.pi / points)
    return (jnp.cos(angles), jnp.sin(angles))


def cells_to_modes(values):
    cos_x, sin_x = tables(X, MX)
    cos_z, sin_z = tables(Z, MZ)
    scaling = 1.0 / math.sqrt(X * Y * Z)
    x_real = contract("syczx,xk->syczk", values, cos_x)
    x_imag = -contract("syczx,xk->syczk", values, sin_x)
    z_real = contract("syczk,zj->kjscy", x_real, cos_z) + contract("syczk,zj->kjscy", x_imag, sin_z)
    z_imag = contract("syczk,zj->kjscy", x_imag, cos_z) - contract("syczk,zj->kjscy", x_real, sin_z)
    mode_shape = (MX * MZ,) + z_real.shape[2:]
    return jnp.stack([z_real.reshape(mode_shape), z_imag.reshape(mode_shape)], axis=3) * scaling


def modes_to_cells(modes):
    cos_x, sin_x = tables(X, MX)
    cos_z, sin_z = tables(Z, MZ)
    scaling = 1.0 / math.sqrt(X * Y * Z)
    by_mode = modes.reshape((MX, MZ) + modes.shape[1:])
    real_part = by_mode[:, :, :, :, 0]
    imag_part = by_mode[:, :, :, :, 1]
    z_real = contract("kjscy,zj->syczk", real_part, cos_z) - contract(
        "kjscy,zj->syczk", imag_part, sin_z
    )
    z_imag = contract("kjscy,zj->syczk", imag_part, cos_z) + contract(
        "kjscy,zj->syczk", real_part, sin_z
    )
    return (
        contract("syczk,xk->syczx", z_real, cos_x) - contract("syczk,xk->syczx", z_imag, sin_x)
    ) * scaling


def forward_y(values, cos_y, sin_y):
    real_part = values[:, :, :, 0]
    imag_part = values[:, :, :, 1]
    out_real = contract("mscy,yq->mscq", real_part, cos_y) + contract(
        "mscy,yq->mscq", imag_part, sin_y
    )
    out_imag = contract("mscy,yq->mscq", imag_part, cos_y) - contract(
        "mscy,yq->mscq", real_part, sin_y
    )
    return jnp.stack([out_real, out_imag], axis=3)


def inverse_y(values, cos_y, sin_y):
    real_part = values[:, :, :, 0]
    imag_part = values[:, :, :, 1]
    out_real = contract("mscq,yq->mscy", real_part, cos_y) - contract(
        "mscq,yq->mscy", imag_part, sin_y
    )
    out_imag = contract("mscq,yq->mscy", imag_part, cos_y) + contract(
        "mscq,yq->mscy", real_part, sin_y
    )
    return jnp.stack([out_real, out_imag], axis=3)


def to_spectrum(local_modes):
    cos_y, sin_y = tables(Y, MY)
    gathered = lax.all_to_all(local_modes, "pencil", split_axis=0, concat_axis=4, tiled=True)
    return forward_y(gathered, cos_y, sin_y)


def from_spectrum(spectrum):
    cos_y, sin_y = tables(Y, MY)
    inverted = inverse_y(spectrum, cos_y, sin_y)
    return lax.all_to_all(inverted, "pencil", split_axis=4, concat_axis=0, tiled=True)


def mix(spectrum, weight):
    a_real = spectrum[:, :, :, 0]
    a_imag = spectrum[:, :, :, 1]
    w_real = weight[:, 0]
    w_imag = weight[:, 1]
    b_real = contract("msiq,mioq->msoq", a_real, w_real) - contract(
        "msiq,mioq->msoq", a_imag, w_imag
    )
    b_imag = contract("msiq,mioq->msoq", a_real, w_imag) + contract(
        "msiq,mioq->msoq", a_imag, w_real
    )
    return jnp.stack([b_real, b_imag], axis=3)


def mix_adjoint(grad_modes, weight):
    g_real = grad_modes[:, :, :, 0]
    g_imag = grad_modes[:, :, :, 1]
    w_real = weight[:, 0]
    w_imag = weight[:, 1]
    a_real = contract("msoq,mioq->msiq", g_real, w_real) + contract(
        "msoq,mioq->msiq", g_imag, w_imag
    )
    a_imag = contract("msoq,mioq->msiq", g_imag, w_real) - contract(
        "msoq,mioq->msiq", g_real, w_imag
    )
    return jnp.stack([a_real, a_imag], axis=3)


def weight_term(spectrum, grad_modes):
    a_real = spectrum[:, :, :, 0]
    a_imag = spectrum[:, :, :, 1]
    g_real = grad_modes[:, :, :, 0]
    g_imag = grad_modes[:, :, :, 1]
    d_real = contract("msiq,msoq->mioq", a_real, g_real) + contract(
        "msiq,msoq->mioq", a_imag, g_imag
    )
    d_imag = contract("msiq,msoq->mioq", a_real, g_imag) - contract(
        "msiq,msoq->mioq", a_imag, g_real
    )
    return jnp.stack([d_real, d_imag], axis=1)


def shards(state_field, spectral_weight, local_weight, channel_bias, cotangent):
    spectrum = to_spectrum(cells_to_modes(state_field))
    spectral_part = modes_to_cells(from_spectrum(mix(spectrum, spectral_weight)))
    pre_act = (
        spectral_part
        + contract("syczx,co->syozx", state_field, local_weight)
        + channel_bias[None, None, :, None, None]
    )
    inner_value = gelu_scale * (pre_act + cubic_term * pre_act * pre_act * pre_act)
    tanh_value = jnp.tanh(inner_value)
    layer_out = 0.5 * pre_act * (1.0 + tanh_value)
    slope_value = 0.5 * (1.0 + tanh_value) + 0.5 * pre_act * (
        1.0 - tanh_value * tanh_value
    ) * gelu_scale * (1.0 + 3.0 * cubic_term * pre_act * pre_act)
    grad_pre = cotangent * slope_value
    grad_modes = to_spectrum(cells_to_modes(grad_pre))
    grad_spectral = lax.psum(weight_term(spectrum, grad_modes), "batch")
    back_cells = modes_to_cells(from_spectrum(mix_adjoint(grad_modes, spectral_weight)))
    grad_state = back_cells + contract("syozx,co->syczx", grad_pre, local_weight)
    local_term = contract("syczx,syozx->co", state_field, grad_pre)
    bias_term = jnp.sum(grad_pre, axis=(0, 1, 3, 4))
    local_total, bias_total = lax.psum((local_term, bias_term), ("batch", "pencil"))
    scaling = 1.0 / math.sqrt(state_field.shape[0] * lax.axis_size("batch") * X * Y * Z)
    return (layer_out, grad_state, grad_spectral, local_total * scaling, bias_total * scaling)


def solution(mesh):
    return jax.shard_map(
        shards,
        mesh=mesh,
        in_specs=(
            P("batch", "pencil", None, None, None),
            P("pencil", None, None, None, None),
            P(),
            P(),
            P("batch", "pencil", None, None, None),
        ),
        out_specs=(
            P("batch", "pencil", None, None, None),
            P("batch", "pencil", None, None, None),
            P("pencil", None, None, None, None),
            P(),
            P(),
        ),
        check_vma=False,
    )
```

profile of v0, /device:TPU:0, one launch (start us, length us, event | category | flops | bytes accessed | tf_op | source)
XLA Modules:
  0.0 1371.1 jit_solution(13904809813645145643)
XLA Ops:
  7.2 69.0 %negate_bitcast_fusion = f32[2,16,32,32,16]{3,4,2,1,0:T(8,128)S(1)} fusion(f32[2,16,32,32,128]{4,3,2,1,0:T(8,128)} %param.5, s32[16]{0:T(128)S(1)} %compare_select_fusion), kind=kOutput, calls=%fused_computation.32 | convolution fusion | flops 805859328 | bytes 18874432 | tf_op jit(solution)/shard_map/syczx,xk->syczk/dot_general | solution.py:21
  76.3 45.2 %fusion.34 = f32[8,2,16,32,16]{3,0,4,2,1:T(8,128)S(1)} fusion(f32[2,16,32,32,16]{3,4,2,1,0:T(8,128)S(1)} %negate_bitcast_fusion, s32[8]{0:T(128)S(1)} %compare_select_fusion.1), kind=kOutput, calls=%fused_computation.41 | convolution fusion | flops 50335232 | bytes 2621472 | tf_op jit(solution)/shard_map/syczk,zj->kjscy/dot_general | solution.py:21
  121.5 32.6 %fusion.36 = f32[8,2,16,32,16]{3,0,4,2,1:T(8,128)S(1)} fusion(f32[2,16,32,32,16]{3,4,2,1,0:T(8,128)S(1)} %negate_bitcast_fusion, s32[8]{0:T(128)S(1)} %compare_select_fusion.1), kind=kOutput, calls=%fused_computation.43 | convolution fusion | flops 50335232 | bytes 2621472 | tf_op jit(solution)/shard_map/syczk,zj->kjscy/dot_general | solution.py:21
  154.1 65.9 %convolution_bitcast_fusion = f32[2,16,32,32,16]{3,4,2,1,0:T(8,128)S(1)} fusion(f32[2,16,32,32,128]{4,3,2,1,0:T(8,128)S(1)} %bitcast.323, s32[16]{0:T(128)S(1)} %compare_select_fusion), kind=kOutput, calls=%fused_computation.80 | convolution fusion | flops 805335040 | bytes 18874432 | tf_op jit(solution)/shard_map/syczx,xk->syczk/dot_general | solution.py:21
  220.0 32.9 %subtract_bitcast_fusion.2 = f32[128,2,32,1,16]{2,0,4,1,3:T(8,128)S(1)} fusion(f32[8,2,16,32,16]{3,0,4,2,1:T(8,128)S(1)} %fusion.34, f32[2,16,32,32,16]{3,4,2,1,0:T(8,128)S(1)} %convolution_bitcast_fusion, s32[8]{0:T(128)S(1)} %compare_select_fusion.1), kind=kOutput, calls=%fused_computation.87 | convolution fusion | flops 50466304 | bytes 3145760 | tf_op jit(solution)/shard_map/syczk,zj->kjscy/dot_general | solution.py:21
  252.9 33.1 %add_bitcast_fusion.2 = f32[128,2,32,1,16]{2,0,4,1,3:T(8,128)S(1)} fusion(f32[8,2,16,32,16]{3,0,4,2,1:T(8,128)S(1)} %fusion.36, f32[2,16,32,32,16]{3,4,2,1,0:T(8,128)S(1)} %convolution_bitcast_fusion, s32[8]{0:T(128)S(1)} %compare_select_fusion.1), kind=kOutput, calls=%fused_computation.88 | convolution fusion | flops 50466304 | bytes 3145760 | tf_op jit(solution)/shard_map/syczk,zj->kjscy/dot_general | solution.py:21
  291.1 4.8 reshape.46
  296.0 5.3 all-to-all-start
  301.3 7.6 fusion.398
  308.9 7.6 all-to-all-done
  340.8 5.0 fusion.93
  358.9 6.5 reshape.48
  369.2 30.5 %fusion.12 = f32[32,2,16,32,128]{4,0,3,2,1:T(8,128)} fusion(f32[2,16,32,32,128]{4,3,2,1,0:T(8,128)} %param.5, f32[32,32]{1,0:T(8,128)S(1)} %copy-done), kind=kOutput, calls=%fused_computation.16 | convolution fusion | flops 1610612736 | bytes 33558528 | tf_op jit(solution)/shard_map/syczx,co->syozx/dot_general | solution.py:21
  402.9 5.5 reshape.49
  419.8 17.5 %fusion.54 = f32[32,16,2,32,16]{0,1,3,4,2:T(8,128)} fusion(f32[16,8,2,32,1,16]{0,1,3,5,2,4:T(8,128)} %copy.312, s32[8]{0:T(128)S(1)} %compare_select_fusion.1), kind=kOutput, calls=%fused_computation.61 | convolution fusion | flops 50335232 | bytes 2621472 | tf_op jit(solution)/shard_map/kjscy,zj->syczk/dot_general | solution.py:21
  437.3 16.0 %fusion.56 = f32[32,16,2,32,16]{0,1,3,4,2:T(8,128)} fusion(f32[16,8,2,32,1,16]{0,1,3,5,2,4:T(8,128)S(1)} %copy-done.8, s32[8]{0:T(128)S(1)} %compare_select_fusion.1), kind=kOutput, calls=%fused_computation.63 | convolution fusion | flops 50335232 | bytes 2621472 | tf_op jit(solution)/shard_map/kjscy,zj->syczk/dot_general | solution.py:21
  456.4 15.4 %fusion.58 = f32[32,16,2,32,16]{0,1,3,4,2:T(8,128)S(1)} fusion(f32[16,8,2,32,1,16]{0,1,3,5,2,4:T(8,128)} %copy.311, s32[8]{0:T(128)S(1)} %compare_select_fusion.1), kind=kOutput, calls=%fused_computation.65 | convolution fusion | flops 50335232 | bytes 2621472 | tf_op jit(solution)/shard_map/kjscy,zj->syczk/dot_general | solution.py:21
  471.9 15.8 %fusion.60 = f32[32,16,2,32,16]{0,1,3,4,2:T(8,128)} fusion(f32[16,8,2,32,1,16]{0,1,3,5,2,4:T(8,128)S(1)} %copy-done.9, s32[8]{0:T(128)S(1)} %compare_select_fusion.1), kind=kOutput, calls=%fused_computation.67 | convolution fusion | flops 50335232 | bytes 2621472 | tf_op jit(solution)/shard_map/kjscy,zj->syczk/dot_general | solution.py:21
  487.7 29.3 %fusion.18 = f32[2,16,32,32,128]{4,3,2,1,0:T(8,128)} fusion(f32[32,16,2,32,16]{0,1,3,4,2:T(8,128)S(1)} %bitcast.327, f32[32,16,2,32,16]{0,1,3,4,2:T(8,128)S(1)} %fusion.58, s32[16]{0:T(128)S(1)} %compare_select_fusion), kind=kOutput, calls=%fused_computation.24 | convolution fusion | flops 805859328 | bytes 20971584 | tf_op jit(solution)/shard_map/syczk,xk->syczx/dot_general | solution.py:21
  517.0 49.6 %fusion.396 = (f32[32]{0:T(128)S(1)}, f32[2,16,32,32,128]{4,3,2,1,0:T(8,128)S(1)}, f32[2,16,32,32,128]{4,3,2,1,0:T(8,128)}) fusion(f32[2,16,32,32,128]{4,3,2,1,0:T(8,128)} %param.9, f32[32]{0:T(128)S(1)} %copy-done.16, f32[32,2,16,32,128]{4,0,3,2,1:T(8,128)} %fusion.12, f32[2,16,32,32,128]{4,3,2,1,0:T(8,128)} %fusion.18, s32[16]{0:T(128)S(1)} %compare_select_fusion, ...), kind=kOutput, calls=%fused_computation.379 | convolution fusion | flops 906522624 | bytes 88080704 | tf_op jit(solution)/shard_map/syczk,xk->syczx/dot_general | solution.py:21
  566.6 33.9 %fusion.102 = f32[32,32]{0,1:T(8,128)S(1)} fusion(f32[2,16,32,32,128]{4,3,2,1,0:T(8,128)} %param.5, f32[2,16,32,32,128]{4,3,2,1,0:T(8,128)S(1)} %get-tuple-element.33), kind=kOutput, calls=%fused_computation.117 | convolution fusion | flops 1610612736 | bytes 33558528 | tf_op jit(solution)/shard_map/syczx,syozx->co/dot_general | solution.py:21
  600.5 68.1 %convolution_negate_fusion = f32[2,16,32,32,16]{3,4,2,1,0:T(8,128)S(1)} fusion(f32[2,16,32,32,128]{4,3,2,1,0:T(8,128)S(1)} %get-tuple-element.33, s32[16]{0:T(128)S(1)} %compare_select_fusion), kind=kOutput, calls=%fused_computation.79 | convolution fusion | flops 805859328 | bytes 18874432 | tf_op jit(solution)/shard_map/syczx,xk->syczk/dot_general | solution.py:21
  668.6 34.1 %fusion.26 = f32[8,2,16,32,16]{3,0,4,2,1:T(8,128)} fusion(f32[2,16,32,32,16]{3,4,2,1,0:T(8,128)S(1)} %convolution_negate_fusion, s32[8]{0:T(128)S(1)} %compare_select_fusion.1), kind=kOutput, calls=%fused_computation.33 | convolution fusion | flops 50335232 | bytes 2621472 | tf_op jit(solution)/shard_map/syczk,zj->kjscy/dot_general | solution.py:21
  702.7 32.6 %fusion.28 = f32[8,2,16,32,16]{3,0,4,2,1:T(8,128)S(1)} fusion(f32[2,16,32,32,16]{3,4,2,1,0:T(8,128)S(1)} %convolution_negate_fusion, s32[8]{0:T(128)S(1)} %compare_select_fusion.1), kind=kOutput, calls=%fused_computation.35 | convolution fusion | flops 50335232 | bytes 2621472 | tf_op jit(solution)/shard_map/syczk,zj->kjscy/dot_general | solution.py:21
  735.3 67.9 %fusion.143 = f32[2,16,32,32,16]{3,4,2,1,0:T(8,128)} fusion(f32[2,16,32,32,128]{4,3,2,1,0:T(8,128)S(1)} %get-tuple-element.33, s32[16]{0:T(128)S(1)} %compare_select_fusion), kind=kOutput, calls=%fused_computation.159 | convolution fusion | flops 805335040 | bytes 18874432 | tf_op jit(solution)/shard_map/syczx,xk->syczk/dot_general | solution.py:21
  803.1 41.1 %all-reduce = (f32[32,32]{0,1:T(8,128)S(1)}, f32[32]{0:T(128)S(1)}) all-reduce(f32[32,32]{0,1:T(8,128)S(1)} %fusion.102, f32[32]{0:T(128)S(1)} %get-tuple-element.32), channel_id=1, replica_groups=mesh['batch'=4,'pencil'=8] {'batch','pencil'}, use_global_device_ids=true, to_apply=%region_1.2 | all-reduce | flops 1056 | bytes 8448 | tf_op jit(solution)/shard_map/psum | solution.py:164
  845.5 36.3 %subtract_bitcast_fusion.1 = f32[128,2,32,1,16]{2,0,4,1,3:T(8,128)S(1)} fusion(f32[8,2,16,32,16]{3,0,4,2,1:T(8,128)} %fusion.26, f32[2,16,32,32,16]{3,4,2,1,0:T(8,128)} %fusion.143, s32[8]{0:T(128)S(1)} %compare_select_fusion.1), kind=kOutput, calls=%fused_computation.85 | convolution fusion | flops 50466304 | bytes 3145760 | tf_op jit(solution)/shard_map/syczk,zj->kjscy/dot_general | solution.py:21
  881.8 32.7 %add_bitcast_fusion.1 = f32[128,2,32,1,16]{2,0,4,1,3:T(8,128)S(1)} fusion(f32[8,2,16,32,16]{3,0,4,2,1:T(8,128)S(1)} %fusion.28, f32[2,16,32,32,16]{3,4,2,1,0:T(8,128)S(1)} %copy-done.2, s32[8]{0:T(128)S(1)} %compare_select_fusion.1), kind=kOutput, calls=%fused_computation.86 | convolution fusion | flops 50466304 | bytes 3145760 | tf_op jit(solution)/shard_map/syczk,zj->kjscy/dot_general | solution.py:21
  919.7 4.9 reshape.50
  928.2 33.4 %fusion.9 = f32[2,16,32,128,32]{3,4,2,1,0:T(8,128)} fusion(f32[2,16,32,32,128]{4,3,2,1,0:T(8,128)} %copy-done.1, f32[32,32]{1,0:T(8,128)S(1)} %copy-done), kind=kOutput, calls=%fused_computation.13 | convolution fusion | flops 1610612736 | bytes 33558528 | tf_op jit(solution)/shard_map/syozx,co->syczx/dot_general | solution.py:21
  974.7 7.7 fusion.63
  982.4 8.3 fusion.125
  992.0 7.5 fusion.62
  999.5 8.6 fusion.119
  1008.2 7.5 fusion.95
  1015.7 7.7 fusion.97
  1032.0 6.6 reshape.52
  1042.8 8.9 add_bitcast_fusion
  1051.7 6.9 subtract_bitcast_fusion
  1066.1 5.9 reshape.53
  1083.4 17.3 %fusion.46 = f32[32,16,2,32,16]{0,1,3,4,2:T(8,128)} fusion(f32[16,8,2,32,1,16]{0,1,3,5,2,4:T(8,128)} %copy.316, s32[8]{0:T(128)S(1)} %compare_select_fusion.1), kind=kOutput, calls=%fused_computation.53 | convolution fusion | flops 50335232 | bytes 2621472 | tf_op jit(solution)/shard_map/kjscy,zj->syczk/dot_general | solution.py:21
  1100.7 15.8 %fusion.48 = f32[32,16,2,32,16]{0,1,3,4,2:T(8,128)} fusion(f32[16,8,2,32,1,16]{0,1,3,5,2,4:T(8,128)S(1)} %copy-done.10, s32[8]{0:T(128)S(1)} %compare_select_fusion.1), kind=kOutput, calls=%fused_computation.55 | convolution fusion | flops 50335232 | bytes 2621472 | tf_op jit(solution)/shard_map/kjscy,zj->syczk/dot_general | solution.py:21
  1119.7 17.6 %fusion.50 = f32[32,16,2,32,16]{0,1,3,4,2:T(8,128)} fusion(f32[16,8,2,32,1,16]{0,1,3,5,2,4:T(8,128)} %copy.315, s32[8]{0:T(128)S(1)} %compare_select_fusion.1), kind=kOutput, calls=%fused_computation.57 | convolution fusion | flops 50335232 | bytes 2621472 | tf_op jit(solution)/shard_map/kjscy,zj->syczk/dot_general | solution.py:21
  1137.2 15.8 %fusion.52 = f32[32,16,2,32,16]{0,1,3,4,2:T(8,128)} fusion(f32[16,8,2,32,1,16]{0,1,3,5,2,4:T(8,128)S(1)} %copy-done.7, s32[8]{0:T(128)S(1)} %compare_select_fusion.1), kind=kOutput, calls=%fused_computation.59 | convolution fusion | flops 50335232 | bytes 2621472 | tf_op jit(solution)/shard_map/kjscy,zj->syczk/dot_general | solution.py:21
  1153.0 29.9 %fusion.14 = f32[2,16,32,32,128]{4,3,2,1,0:T(8,128)S(1)} fusion(f32[32,16,2,32,16]{0,1,3,4,2:T(8,128)} %fusion.46, f32[32,16,2,32,16]{0,1,3,4,2:T(8,128)} %fusion.50, s32[16]{0:T(128)S(1)} %compare_select_fusion), kind=kOutput, calls=%fused_computation.20 | convolution fusion | flops 805859328 | bytes 20971584 | tf_op jit(solution)/shard_map/syczk,xk->syczx/dot_general | solution.py:21
  1183.0 38.7 %bitcast_add_fusion = f32[2,16,32,32,128]{4,3,2,1,0:T(8,128)} fusion(f32[2,16,32,128,32]{3,4,2,1,0:T(8,128)S(1)} %bitcast.325, f32[2,16,32,32,128]{4,3,2,1,0:T(8,128)S(1)} %fusion.14, f32[32,16,2,32,16]{0,1,3,4,2:T(8,128)} %fusion.52, f32[32,16,2,32,16]{0,1,3,4,2:T(8,128)} %fusion.48, s32[16]{0:T(128)S(1)} %compare_select_fusion), kind=kOutput, calls=%fused_computation.8 | convolution fusion | flops 818442240 | bytes 54526016 | tf_op jit(solution)/shard_map/syczk,xk->syczx/dot_general | solution.py:21
  1221.7 132.7 %all-reduce.3.cloned.1.call-done = f32[16,2,32,32,16]{2,3,4,0,1:T(8,128)} async-done(((f32[16,2,32,32,16]{2,3,4,0,1:T(8,128)}), f32[16,2,32,32,16]{2,3,4,0,1:T(8,128)}) %all-reduce.3.cloned.1.call-update) | async-done | bytes 2097168 | tf_op jit(solution)/shard_map/psum | solution.py:159
  1354.4 9.7 copy.293
  (124 shorter events, 123.0 us)
Async XLA Ops:
  7.2 362.0 %copy-start = (f32[32,32]{1,0:T(8,128)S(1)}, f32[32,32]{1,0:T(8,128)}, u32[]{:S(2)}) copy-start(f32[32,32]{1,0:T(8,128)} %param.7) | copy-start | bytes 12292
  7.2 146.8 %slice-start = ((s8[16777216]{0:T(1024)(128)(4,1)}), s8[4194304]{0:T(1024)(128)(4,1)S(1)}, s32[]{:S(2)}) async-start(s8[16777216]{0:T(1024)(128)(4,1)} %bitcast.322), calls=%async_computation.5 | async-start | bytes 8388608
  7.2 146.8 %slice-start.1 = ((s8[16777216]{0:T(1024)(128)(4,1)}), s8[4194304]{0:T(1024)(128)(4,1)S(1)}, s32[]{:S(2)}) async-start(s8[16777216]{0:T(1024)(128)(4,1)} %bitcast.322), calls=%async_computation.6 | async-start | bytes 8388608
  7.2 146.8 %slice-start.2 = ((s8[16777216]{0:T(1024)(128)(4,1)}), s8[4194304]{0:T(1024)(128)(4,1)S(1)}, s32[]{:S(2)}) async-start(s8[16777216]{0:T(1024)(128)(4,1)} %bitcast.322), calls=%async_computation.7 | async-start | bytes 8388608
  76.3 77.8 %slice-start.3 = ((s8[16777216]{0:T(1024)(128)(4,1)}), s8[4194304]{0:T(1024)(128)(4,1)S(1)}, s32[]{:S(2)}) async-start(s8[16777216]{0:T(1024)(128)(4,1)} %bitcast.322), calls=%async_computation.8 | async-start | bytes 8388608
  296.0 20.6 %all-to-all-start = ((f32[8,1,32768]{2,1,0:T(1,128)}), f32[8,1,32768]{2,1,0:T(1,128)S(1)}, u32[]{:S(2)}, u32[]{:S(2)}) async-start(f32[8,1,32768]{2,1,0:T(1,128)} %reshape.46), calls=%async_computation | async-start | bytes 2097152 | tf_op jit(solution)/shard_map/all_to_all | solution.py:91
  327.7 3.8 copy-start.5
  330.2 15.6 %copy-start.12 = (f32[16,2,32,16]{2,3,1,0:T(8,128)}, f32[16,2,32,16]{2,3,1,0:T(8,128)S(1)}, u32[]{:S(2)}) copy-start(f32[16,2,32,16]{2,3,1,0:T(8,128)S(1)} %fusion.101) | copy-start | bytes 196612
  331.5 9.3 copy-start.14
  331.5 9.3 copy-start.3
  365.5 34.3 %all-to-all-start.1 = ((f32[8,1,32768]{2,1,0:T(1,128)}), f32[8,1,32768]{2,1,0:T(1,128)S(1)}, u32[]{:S(2)}, u32[]{:S(2)}) async-start(f32[8,1,32768]{2,1,0:T(1,128)} %reshape.48), calls=%async_computation.1 | async-start | bytes 2097152 | tf_op jit(solution)/shard_map/all_to_all | solution.py:98
  419.8 17.5 %copy-start.8 = (f32[16,8,2,32,1,16]{0,1,3,5,2,4:T(8,128)S(1)}, f32[16,8,2,32,1,16]{0,1,3,5,2,4:T(8,128)}, u32[]{:S(2)}) copy-start(f32[16,8,2,32,1,16]{0,1,3,5,2,4:T(8,128)} %copy.312) | copy-start | bytes 1572868
  456.4 15.5 %copy-start.9 = (f32[16,8,2,32,1,16]{0,1,3,5,2,4:T(8,128)S(1)}, f32[16,8,2,32,1,16]{0,1,3,5,2,4:T(8,128)}, u32[]{:S(2)}) copy-start(f32[16,8,2,32,1,16]{0,1,3,5,2,4:T(8,128)} %copy.311) | copy-start | bytes 1572868
  456.4 31.3 %slice-start.8 = ((s8[8388608]{0:T(1024)(128)(4,1)}), s8[4194304]{0:T(1024)(128)(4,1)S(1)}, s32[]{:S(2)}) async-start(s8[8388608]{0:T(1024)(128)(4,1)} %bitcast.326), calls=%async_computation.13 | async-start | bytes 8388608
  471.9 15.8 %slice-start.9 = ((s8[8388608]{0:T(1024)(128)(4,1)}), s8[4194304]{0:T(1024)(128)(4,1)S(1)}, s32[]{:S(2)}) async-start(s8[8388608]{0:T(1024)(128)(4,1)} %bitcast.326), calls=%async_computation.14 | async-start | bytes 8388608
  471.9 45.1 %slice-start.10 = ((s8[8388608]{0:T(1024)(128)(4,1)}), s8[4194304]{0:T(1024)(128)(4,1)S(1)}, s32[]{:S(2)}) async-start(s8[8388608]{0:T(1024)(128)(4,1)} %bitcast.346), calls=%async_computation.15 | async-start | bytes 8388608
  487.7 29.3 %slice-start.11 = ((s8[8388608]{0:T(1024)(128)(4,1)}), s8[4194304]{0:T(1024)(128)(4,1)S(1)}, s32[]{:S(2)}) async-start(s8[8388608]{0:T(1024)(128)(4,1)} %bitcast.346), calls=%async_computation.16 | async-start | bytes 8388608
  487.7 29.3 %copy-start.16 = (f32[32]{0:T(128)S(1)}, f32[32]{0:T(128)}, u32[]{:S(2)}) copy-start(f32[32]{0:T(128)} %param.8) | copy-start | bytes 388
  566.6 168.6 %copy-start.1 = (f32[2,16,32,32,128]{4,3,2,1,0:T(8,128)}, f32[2,16,32,32,128]{4,3,2,1,0:T(8,128)S(1)}, u32[]{:S(2)}) copy-start(f32[2,16,32,32,128]{4,3,2,1,0:T(8,128)S(1)} %get-tuple-element.33) | copy-start | bytes 50331652
  845.5 36.3 %copy-start.2 = (f32[2,16,32,32,16]{3,4,2,1,0:T(8,128)S(1)}, f32[2,16,32,32,16]{3,4,2,1,0:T(8,128)}, u32[]{:S(2)}) copy-start(f32[2,16,32,32,16]{3,4,2,1,0:T(8,128)} %fusion.143) | copy-start | bytes 6291460
  924.5 37.0 %all-to-all-start.2 = ((f32[8,1,32768]{2,1,0:T(1,128)}), f32[8,1,32768]{2,1,0:T(1,128)S(1)}, u32[]{:S(2)}, u32[]{:S(2)}) async-start(f32[8,1,32768]{2,1,0:T(1,128)} %reshape.50), calls=%async_computation.2 | async-start | bytes 2097152 | tf_op jit(solution)/shard_map/all_to_all | solution.py:91
  970.9 3.8 copy-start.6
  973.4 9.0 copy-start.15
  992.0 16.2 %copy-start.4 = (f32[16,1,32,32,16]{3,4,2,1,0:T(8,128)S(1)}, f32[16,1,32,32,16]{3,4,2,1,0:T(8,128)}, u32[]{:S(2)}) copy-start(f32[16,1,32,32,16]{3,4,2,1,0:T(8,128)} %get-tuple-element.35) | copy-start | bytes 3145732
  1032.0 10.8 copy-start.13
  1038.5 24.4 %all-to-all-start.3 = ((f32[8,1,32768]{2,1,0:T(1,128)}), f32[8,1,32768]{2,1,0:T(1,128)S(1)}, u32[]{:S(2)}, u32[]{:S(2)}) async-start(f32[8,1,32768]{2,1,0:T(1,128)} %reshape.52), calls=%async_computation.3 | async-start | bytes 2097152 | tf_op jit(solution)/shard_map/all_to_all | solution.py:98
  1042.7 311.7 %all-reduce.3.cloned.1.call-start = ((), (), s32[]{:S(2)}) async-start(), calls=%async_computation.4 | async-start | bytes 16777216 | tf_op jit(solution)/shard_map/psum | solution.py:159
  1042.8 8.9 copy-start.11
  1083.4 17.3 %copy-start.10 = (f32[16,8,2,32,1,16]{0,1,3,5,2,4:T(8,128)S(1)}, f32[16,8,2,32,1,16]{0,1,3,5,2,4:T(8,128)}, u32[]{:S(2)}) copy-start(f32[16,8,2,32,1,16]{0,1,3,5,2,4:T(8,128)} %copy.316) | copy-start | bytes 1572868
  1119.7 17.6 %copy-start.7 = (f32[16,8,2,32,1,16]{0,1,3,5,2,4:T(8,128)S(1)}, f32[16,8,2,32,1,16]{0,1,3,5,2,4:T(8,128)}, u32[]{:S(2)}) copy-start(f32[16,8,2,32,1,16]{0,1,3,5,2,4:T(8,128)} %copy.315) | copy-start | bytes 1572868
  1137.2 45.7 %slice-start.4 = ((s8[16777216]{0:T(1024)(128)(4,1)}), s8[4194304]{0:T(1024)(128)(4,1)S(1)}, s32[]{:S(2)}) async-start(s8[16777216]{0:T(1024)(128)(4,1)} %bitcast.324), calls=%async_computation.9 | async-start | bytes 8388608
  1153.0 29.9 %slice-start.5 = ((s8[16777216]{0:T(1024)(128)(4,1)}), s8[4194304]{0:T(1024)(128)(4,1)S(1)}, s32[]{:S(2)}) async-start(s8[16777216]{0:T(1024)(128)(4,1)} %bitcast.324), calls=%async_computation.10 | async-start | bytes 8388608
  1153.0 30.0 %slice-start.6 = ((s8[16777216]{0:T(1024)(128)(4,1)}), s8[4194304]{0:T(1024)(128)(4,1)S(1)}, s32[]{:S(2)}) async-start(s8[16777216]{0:T(1024)(128)(4,1)} %bitcast.324), calls=%async_computation.11 | async-start | bytes 8388608
  1153.0 30.0 %slice-start.7 = ((s8[16777216]{0:T(1024)(128)(4,1)}), s8[4194304]{0:T(1024)(128)(4,1)S(1)}, s32[]{:S(2)}) async-start(s8[16777216]{0:T(1024)(128)(4,1)} %bitcast.324), calls=%async_computation.12 | async-start | bytes 8388608
Sparse Core Ops, SparseCore 0:
  1063.1 291.2 all-reduce.2
where the time goes:
time: 1380 us; the launch traced here: 1370 us
  matrix products  1030 us (75%)
  waiting for transfers between devices  140 us (10%)
  local copies, waits for them, and re-layouts  108 us (8%)
  blocking collectives  41.1 us (3%)
  other arithmetic  22.9 us (2%)
  starting transfers between devices  16.9 us (1%)
  between operations  14.8 us (1%)
    dot_general x55, matrix products, contract(): return jnp.einsum(form, left, right, precision=lax.Precision.HIGHEST)  1030 us
    psum x1, waiting for transfers between devices, shards(): grad_spectral = lax.psum(weight_term(spectrum, grad_modes), 'batch')  133 us
    unnamed x72, local copies, waits for them, and re-layouts  66.2 us
    psum x1, blocking collectives, shards(): lax.psum((local_term, bias_term), ('batch', 'pencil'))  41.1 us
  transfers between devices with their start and end apart: 5, of which 2 were waited for; matrix products, arithmetic and copies ran while one was open for 18% of the time, Pallas kernels for 0%

commit v1 on v0

v1 whole, which is shorter than its diff:
```python
import functools
import math

import jax
import jax.numpy as jnp
import ml_dtypes
import numpy as np
from jax import lax
from jax.experimental import pallas as pl
from jax.experimental.pallas import tpu as pltpu
from jax.sharding import PartitionSpec as P

X = 128
Y = 128
Z = 32
C = 32
MX = 16
MY = 16
MZ = 8
MODES = MX * MZ
CQ = C * MY
ZJ = 9
ZJP = 10
GX = 4 * X
YB = 4

F32 = jnp.float32
BF16 = jnp.bfloat16
gelu_scale = math.sqrt(2.0 / math.pi)
cubic_term = 0.044715
VMEM_LIMIT = 56 * 1024 * 1024


def np_split(a):
    a = np.asarray(a, np.float32)
    hi = a.astype(ml_dtypes.bfloat16)
    lo = (a - hi.astype(np.float32)).astype(ml_dtypes.bfloat16)
    return hi, lo


def freqs(kept):
    return np.array([j if j < kept // 2 else j - kept for j in range(kept)])


def z_functions():
    z = np.arange(Z)
    rows = [np.cos(2 * np.pi * (j * z % Z) / Z) for j in range(5)]
    rows += [np.sin(2 * np.pi * (j * z % Z) / Z) for j in range(1, 5)]
    rows += [np.ones(Z)]
    return np.stack(rows)


def z_forward_table():
    zt = z_functions().reshape(ZJP, 4, 8)
    t = np.einsum("jab,cd->jcadb", zt, np.eye(8)).reshape(ZJP * 8, 256)
    hi, lo = np_split(t)
    return np.concatenate([hi, lo], 0)


def z_inverse_table():
    zt = z_functions().reshape(ZJP, 4, 8)
    t = np.einsum("jab,cd->acbjd", zt, np.eye(8)).reshape(256, ZJP * 8)
    hi, lo = np_split(t)
    return np.concatenate([hi, hi, lo], 1)


def x_table():
    x = np.arange(X)
    t = np.zeros((2, MX, MZ, ZJ, X))
    for a, fx in enumerate(freqs(MX)):
        cx = np.cos(2 * np.pi * (fx * x % X) / X)
        sx = np.sin(2 * np.pi * (fx * x % X) / X)
        for b, fz in enumerate(freqs(MZ)):
            k = abs(fz)
            t[0, a, b, k] = cx
            t[1, a, b, k] = sx
            if k > 0:
                t[0, a, b, 4 + k] = -np.sign(fz) * sx
                t[1, a, b, 4 + k] = np.sign(fz) * cx
    t = t.reshape(2 * MODES, ZJ * X) / math.sqrt(X * Y * Z)
    hi, lo = np_split(t)
    return np.concatenate([hi, lo], 0)


def channel_group(yl):
    return min(C, max(8, X // yl))


def y_tables(yl):
    cg = channel_group(yl)
    f = freqs(MY)
    ang = 2 * np.pi * (np.arange(yl)[:, None] * f[None, :] % Y) / Y
    t = np.stack([np.cos(ang), np.sin(ang)])
    fwd = np.einsum("tyq,cd->yctdq", t, np.eye(cg)).reshape(yl * cg, 2 * cg * MY)
    inv = np.einsum("tyq,cd->dqtyc", t, np.eye(cg)).reshape(cg * MY, 2 * yl * cg)
    out = []
    for m in (fwd, inv):
        hi, lo = np_split(m)
        out.append(np.concatenate([hi, hi, lo], 0))
    return out


def cell_row(yl, y, g):
    cg = channel_group(yl)
    return (g * 8 // cg) * (yl * cg) + y * cg + g * 8 % cg


def phase_table(yl, pencils):
    f = freqs(MY)
    ang = 2 * np.pi * (np.arange(pencils)[:, None] * yl * f[None, :] % Y) / Y
    t = np.stack([np.cos(ang), np.sin(ang)], 1)
    t = np.tile(t, (1, 4, C))
    return t.astype(np.float32)


def split(v):
    hi = v.astype(BF16)
    lo = (v - hi.astype(F32)).astype(BF16)
    return hi, lo


def dot(a, b):
    return lax.dot_general(a, b, (((1,), (0,)), ((), ())), preferred_element_type=F32)


def dot_nt(a, b):
    return lax.dot_general(a, b, (((1,), (1,)), ((), ())), preferred_element_type=F32)


def dot3(a, bh, bl, f=dot):
    ah, al = split(a)
    return f(ah, bh) + f(al, bh) + f(ah, bl)


def iota(shape, dim):
    return lax.broadcasted_iota(jnp.int32, shape, dim)


def regroup(parts):
    return jnp.concatenate(
        [jnp.concatenate([p[g * 64 : (g + 1) * 64] for p in parts], 0) for g in range(4)], 1
    )


def load_parts(ref, y):
    return [ref[y, :, zo * 8 : (zo + 1) * 8, :].reshape(256, X) for zo in range(4)]


class Rows:
    def __init__(self, source, sample, held, sems):
        self.source, self.sample, self.held, self.sems = source, sample, held, sems
        self.blocks = sems.shape[0]
        self.deep = held.shape[0] // self.blocks

    def copy(self, block):
        rows = pl.ds(block * self.deep, self.deep)
        return pltpu.make_async_copy(
            self.source.at[self.sample, rows], self.held.at[rows], self.sems.at[block]
        )

    def start(self):
        for block in range(self.blocks):
            self.copy(block).start()


def z_forward(his, los, ltf_ref, rk, y):
    gh, gl = regroup(his), regroup(los)
    n = ZJP * 8
    yl = rk.shape[0] // C
    both = dot(ltf_ref[...], gh)
    r = both[:n] + both[n:] + dot(ltf_ref[:n, :], gl)
    for g in range(4):
        rows = pl.ds(pl.multiple_of(cell_row(yl, y, g), 8), 8)
        for j in range(ZJ):
            rk[rows, j * X : (j + 1) * X] = r[j * 8 : (j + 1) * 8, g * X : (g + 1) * X]
    return r[ZJ * 8 :]


def by_group(v, table_ref, group):
    rows, lanes = v.shape
    parts = lanes // group
    v = jnp.concatenate([v[:, k * group : (k + 1) * group] for k in range(parts)], 0)
    hi, lo = split(v)
    r = dot(jnp.concatenate([hi, lo], 1), table_ref[: 2 * group, :])
    r = r + dot(hi, table_ref[2 * group :, :])
    half = r.shape[1] // 2
    return [
        jnp.concatenate(
            [r[k * rows : (k + 1) * rows, t * half : (t + 1) * half] for k in range(parts)], 1
        )
        for t in range(2)
    ]


def to_modes(rk, xt_ref, yf_ref, ph_ref, out_ref):
    rh, rl = split(rk[...])
    both = dot_nt(xt_ref[...], rh)
    n = 2 * MODES
    ab = both[:n] + both[n:] + dot_nt(xt_ref[:n, :], rl)
    zc, zs = by_group(ab, yf_ref, yf_ref.shape[0] // 3)
    re = zc[:MODES] - zs[MODES:]
    im = -(zc[MODES:] + zs[:MODES])
    pc, ps = own_phase(ph_ref)
    groups = out_ref.shape[0]
    mg = MODES // groups
    out_ref[:, :mg, :] = (re * pc + im * ps).reshape(groups, mg, CQ)
    out_ref[:, mg : 2 * mg, :] = (im * pc - re * ps).reshape(groups, mg, CQ)


def from_modes(m_ref, xt_ref, yi_ref, ph_ref, bias_ref, qs):
    groups, rows, _ = m_ref.shape
    mg = rows // 2
    re0 = m_ref[:, :mg, :].reshape(MODES, CQ)
    im0 = m_ref[:, mg:, :].reshape(MODES, CQ)
    pc, ps = own_phase(ph_ref)
    m = jnp.concatenate([re0 * pc - im0 * ps, im0 * pc + re0 * ps], 0)
    zc, zs = by_group(m, yi_ref, yi_ref.shape[0] // 3)
    re = zc[:MODES] - zs[MODES:]
    im = zc[MODES:] + zs[:MODES]
    yt = jnp.concatenate([re, -im], 0).T
    q = dot3(yt, xt_ref[: 2 * MODES, :], xt_ref[2 * MODES :, :])
    n = ZJP * 8
    yl = qs.shape[0]
    for y in range(yl):
        pieces = []
        for j in range(ZJ):
            pieces.append(
                jnp.concatenate(
                    [
                        q[cell_row(yl, y, g) : cell_row(yl, y, g) + 8, j * X : (j + 1) * X]
                        for g in range(4)
                    ],
                    1,
                )
            )
        if bias_ref is None:
            pieces.append(jnp.zeros((8, GX), F32))
        else:
            pieces.append(bias_rows(bias_ref))
        hi, lo = split(jnp.concatenate(pieces, 0))
        qs[y, 0:n, :] = hi
        qs[y, n : 2 * n, :] = lo
        qs[y, 2 * n :, :] = hi


def weight_stack(w_ref, ws, f):
    spread = (iota((256, C), 0) // 8 == iota((256, C), 1)).astype(F32).astype(BF16)
    same = iota((256, 256), 0) % 8 == iota((256, 256), 1) % 8

    def wide(part):
        t = dot_nt(f(spread, part).astype(BF16), spread)
        return jnp.where(same, t, 0.0).astype(BF16)

    hi, lo = split(w_ref[...])
    ws[0:256, :] = wide(hi)
    ws[256:512, :] = wide(lo)


def pointwise(ws, xh, xl):
    both = dot(ws[...], xh)
    return both[:256] + both[256:] + dot(ws[0:256, :], xl)


def bias_rows(b_ref):
    diag = iota((C, C), 0) == iota((C, C), 1)
    col = jnp.sum(jnp.where(diag, b_ref[...], 0.0), axis=1, keepdims=True)
    return jnp.concatenate(
        [jnp.broadcast_to(col[g * 8 : (g + 1) * 8], (8, X)) for g in range(4)], 1
    )


def own_phase(ph_ref):
    own = ph_ref[lax.axis_index("pencil")]
    return own[0:1], own[1:2]


def forward_kernel(s, x_ref, ltf_ref, xt_ref, yf_ref, ph_ref, out_ref, rk, xs, x_sem):
    yb = pl.program_id(0)
    x = Rows(x_ref, s, xs, x_sem)
    deep = x.deep

    @pl.when(yb == 0)
    def _():
        x.start()

    x.copy(yb).wait()

    def step(y, carry):
        hl = [split(p) for p in load_parts(xs, yb * deep + y)]
        z_forward([h for h, _ in hl], [l for _, l in hl], ltf_ref, rk, yb * deep + y)
        return carry

    lax.fori_loop(0, deep, step, 0, unroll=True)

    @pl.when(yb == pl.num_programs(0) - 1)
    def _():
        to_modes(rk, xt_ref, yf_ref, ph_ref, out_ref)


def cell_kernel(
    s, x_ref, ct_ref, m_ref, w_ref, bias_ref, ltf_ref, lti_ref, xt_ref, yf_ref, yi_ref, ph_ref,
    *refs,
):
    out_ref, gp_ref, v_ref, rk, qs, ws, lacc, bacc, xs, x_sem, cts, ct_sem = refs[-12:]
    yb = pl.program_id(0)
    x = Rows(x_ref, s, xs, x_sem)
    ct = Rows(ct_ref, s, cts, ct_sem)
    deep = x.deep

    @pl.when(yb == 0)
    def _():
        x.start()
        ct.start()
        from_modes(m_ref, xt_ref, yi_ref, ph_ref, bias_ref, qs)
        weight_stack(w_ref, ws, dot_nt)
        lacc[...] = jnp.zeros_like(lacc)
        bacc[...] = jnp.zeros_like(bacc)

    x.copy(yb).wait()
    ct.copy(yb).wait()

    def step(y, carry):
        hl = [split(p) for p in load_parts(xs, yb * deep + y)]
        xh = jnp.concatenate([h for h, _ in hl], 1)
        xl = jnp.concatenate([l for _, l in hl], 1)
        conv = pointwise(ws, xh, xl)
        spec = dot(lti_ref[...], qs[yb * deep + y])
        ghs, gls = [], []
        for zo in range(4):
            gs = []
            for g in range(4):
                p = (
                    conv[g * 64 : (g + 1) * 64, zo * X : (zo + 1) * X]
                    + spec[zo * 64 : (zo + 1) * 64, g * X : (g + 1) * X]
                )
                p2 = p * p
                u = p2 * (gelu_scale * cubic_term) + gelu_scale
                t = jnp.tanh(p * u)
                h = 0.5 * t + 0.5
                o = p * h
                d = p2 * (1.5 * gelu_scale * cubic_term) + 0.5 * gelu_scale
                slope = h + p * (1.0 - t * t) * d
                where = (0, y, slice(g * 8, (g + 1) * 8), slice(zo * 8, (zo + 1) * 8))
                out_ref[where] = o.reshape(8, 8, X)
                gp = cts[(yb * deep + y,) + where[2:]].reshape(64, X) * slope
                gp_ref[where] = gp.reshape(8, 8, X)
                gs.append(gp)
            gh, gl = split(jnp.concatenate(gs, 0))
            ghs.append(gh)
            gls.append(gl)
        bacc[...] += z_forward(ghs, gls, ltf_ref, rk, yb * deep + y)
        gh = jnp.concatenate(ghs, 1)
        gl = jnp.concatenate(gls, 1)
        both = dot_nt(jnp.concatenate([xh, xl], 0), gh)
        lacc[...] += both[:256] + both[256:] + dot_nt(xh, gl)
        return carry

    lax.fori_loop(0, deep, step, 0, unroll=True)

    @pl.when(yb == pl.num_programs(0) - 1)
    def _():
        to_modes(rk, xt_ref, yf_ref, ph_ref, v_ref)
        same = iota((256, 256), 0) % 8 == iota((256, 256), 1) % 8
        rest = jnp.where(same, lacc[...], 0.0).reshape(C, 8, 256).sum(axis=1)
        pick = (iota((256, X), 0) // 8 == iota((256, X), 1)).astype(F32).astype(BF16)
        loc = jnp.zeros((C, X), F32)
        for _ in range(3):
            part = rest.astype(BF16)
            loc = loc + dot(part, pick)
            rest = rest - part.astype(F32)
        b = bacc[...]
        col = jnp.concatenate(
            [jnp.sum(b[:, g * X : (g + 1) * X], axis=1, keepdims=True) for g in range(4)], 0
        )
        diag = iota((C, X), 0) + C == iota((C, X), 1)
        row = jnp.sum(jnp.where(diag, col, 0.0), axis=0, keepdims=True)
        loc = loc + row
        loc = jnp.concatenate([loc[g * 8 : (g + 1) * 8] for g in range(4)], 1)
        extra = v_ref.shape[1] - 8
        for d in range(v_ref.shape[0]):
            v_ref[d, extra:, :] = loc


def back_kernel(
    gp_ref, m_ref, w_ref, lti_ref, xt_ref, yi_ref, ph_ref, *refs
):
    out_ref, qs, ws, gps, gp_sem = refs[-5:]
    yb = pl.program_id(0)
    gp = Rows(gp_ref, 0, gps, gp_sem)
    deep = gp.deep

    @pl.when(yb == 0)
    def _():
        gp.start()
        from_modes(m_ref, xt_ref, yi_ref, ph_ref, None, qs)
        weight_stack(w_ref, ws, dot)

    gp.copy(yb).wait()

    def step(y, carry):
        hl = [split(p) for p in load_parts(gps, yb * deep + y)]
        xh = jnp.concatenate([h for h, _ in hl], 1)
        xl = jnp.concatenate([l for _, l in hl], 1)
        conv = pointwise(ws, xh, xl)
        spec = dot(lti_ref[...], qs[yb * deep + y])
        for zo in range(4):
            for g in range(4):
                p = (
                    conv[g * 64 : (g + 1) * 64, zo * X : (zo + 1) * X]
                    + spec[zo * 64 : (zo + 1) * 64, g * X : (g + 1) * X]
                )
                out_ref[0, y, g * 8 : (g + 1) * 8, zo * 8 : (zo + 1) * 8, :] = p.reshape(8, 8, X)
        return carry

    lax.fori_loop(0, deep, step, 0, unroll=True)


def turn_kernel(w_ref, out_ref):
    for m in range(0, w_ref.shape[0], 2):
        four = jnp.concatenate([w_ref[m, 0], w_ref[m, 1], w_ref[m + 1, 0], w_ref[m + 1, 1]], 1)
        out_ref[m : m + 2] = four.T.reshape(2, 2, C, CQ)


def own_lanes(rows):
    return iota((rows, X), 0) % 8 == iota((rows, X), 1) // MY


def lane_period():
    return (iota((2 * X, X), 0) % MY == iota((2 * X, X), 1) % MY).astype(F32).astype(BF16)


def rows_table(r):
    a = np.einsum("gh,rs->grsh", np.eye(4), np.eye(r))
    a = np.repeat(a[..., None], 8, axis=-1).reshape(4 * r, r * C)
    return a.astype(ml_dtypes.bfloat16)


def total_of(ref):
    t = ref[0]
    for d in range(1, ref.shape[0]):
        t = t + ref[d]
    return t


def keep(side_ref, prev_ref, s):
    before = side_ref.shape[0] - s.shape[0]
    if prev_ref is not None:
        side_ref[:before, :] = prev_ref[...]
    side_ref[before:, :] = s


def mix_kernel(v_ref, wt_ref, sum_ref, *refs):
    mixed_ref, side_ref = refs[-2:]
    ml = wt_ref.shape[0]
    r = 2 * ml
    s = total_of(v_ref)
    keep(side_ref, refs[0] if len(refs) > 2 else None, s)

    folds = [None] * r
    for m in range(ml):
        re, im = s[m : m + 1], s[ml + m : ml + m + 1]
        wr, wi = wt_ref[m, 0], wt_ref[m, 1]
        for k, p in enumerate((re * wr - im * wi, re * wi + im * wr)):
            folds[k * ml + m] = (p[:, 0:128] + p[:, 128:256]) + (p[:, 256:384] + p[:, 384:512])
    v = jnp.concatenate(folds, 0)
    v = dot(jnp.concatenate(split(v), 1), lane_period())
    hi, lo = split(jnp.where(own_lanes(r * C), v, 0.0))
    v = dot(sum_ref[...], hi) + dot(sum_ref[...], lo)
    v = jnp.concatenate([v[g * r : (g + 1) * r] for g in range(4)], 1)
    for d in range(mixed_ref.shape[0]):
        mixed_ref[d] = v


def adjoint_kernel(v_ref, wt_ref, sum_ref, *refs):
    back_ref, side_ref = refs[-2:]
    ml = wt_ref.shape[0]
    r = 2 * ml
    s = total_of(v_ref)
    keep(side_ref, refs[0] if len(refs) > 2 else None, s)

    own = own_lanes(8)
    e = jnp.concatenate(
        [
            jnp.where(own, s[k : k + 1, g * X : (g + 1) * X], 0.0)
            for k in range(r)
            for g in range(4)
        ],
        0,
    )
    p = dot(jnp.concatenate(split(e), 1), lane_period())
    folds = [None] * r
    for m in range(ml):
        wr, wi = wt_ref[m, 0], wt_ref[m, 1]
        gr = jnp.concatenate([p[m * C : (m + 1) * C]] * 4, 1)
        gi = jnp.concatenate([p[(ml + m) * C : (ml + m + 1) * C]] * 4, 1)
        for k, v in enumerate((gr * wr + gi * wi, gi * wr - gr * wi)):
            folds[k * ml + m] = (v[0:8] + v[8:16]) + (v[16:24] + v[24:32])
    hi, lo = split(jnp.concatenate(folds, 0))
    ones = (iota((r, 8 * r), 0) == iota((r, 8 * r), 1) // 8).astype(F32).astype(BF16)
    v = dot(ones, hi) + dot(ones, lo)
    for d in range(back_ref.shape[0]):
        back_ref[d] = v


def weight_kernel(scaling, samples, *refs):
    gw_ref, local_ref, bias_ref, sides = refs[-4:]
    mb = gw_ref.shape[0]
    batches = sides.shape[0]
    rows = (sides.shape[1] // samples - 8) // 2
    ml = rows // 2

    @pl.when(pl.program_id(0) == 0)
    def _():
        for k in range(batches):
            at = lax.rem(lax.axis_index("batch") + batches - k, batches)
            sides[at] = refs[k][...]

    own = own_lanes(8)
    period = lane_period()
    pairs = [(s, b) for s in range(samples) for b in range(batches)]

    def spec_row(s, b, at):
        at = s * rows + at
        return sides[b, at : at + 1, :]

    def grad_row(s, b, at):
        at = samples * rows + s * (rows + 8) + at
        return sides[b, at : at + 1, :]

    def periodic(m):
        rows = [grad_row(s, b, at) for s, b in pairs for at in (m, ml + m)]
        e = jnp.concatenate(
            [jnp.where(own, r[:, g * X : (g + 1) * X], 0.0) for r in rows for g in range(4)], 0
        )
        return dot(jnp.concatenate(split(e), 1), period)

    def gradient(m):
        p = periodic(m)
        rr = [[None] * 4 for _ in range(2)]
        for k, (s, b) in enumerate(pairs):
            gr = p[2 * C * k : 2 * C * k + C]
            gi = p[2 * C * k + C : 2 * C * (k + 1)]
            ar, ai = spec_row(s, b, m), spec_row(s, b, ml + m)
            for g in range(4):
                cr, ci = ar[:, g * X : (g + 1) * X], ai[:, g * X : (g + 1) * X]
                for t, v in enumerate((cr * gr + ci * gi, cr * gi - ci * gr)):
                    rr[t][g] = v if rr[t][g] is None else rr[t][g] + v
        return [jnp.concatenate(r, 1) for r in rr]

    for c in range(ml // mb):

        @pl.when(pl.program_id(0) == c)
        def _():
            for k in range(0, mb, 2):
                m = c * mb + k
                v = jnp.concatenate(gradient(m) + gradient(m + 1), 0).T
                for t in range(4):
                    gw_ref[k + t // 2, t % 2] = v[:, t * C : (t + 1) * C]

    @pl.when(pl.program_id(0) == 0)
    def _():
        t = jnp.zeros((8, CQ), F32)
        for s, b in pairs:
            at = samples * rows + (s + 1) * (rows + 8)
            t = t + sides[b, at - 8 : at, :]
        t = jnp.concatenate([t[:, g * X : (g + 1) * X] for g in range(4)], 0) * scaling
        local_ref[...] = t[:, :C]
        bias_ref[...] = pltpu.roll(t, X - C, 1)[0:1, :C]


def whole(shape):
    return pl.BlockSpec(shape, lambda *_: (0,) * len(shape))


def params():
    return pltpu.CompilerParams(vmem_limit_bytes=VMEM_LIMIT)


def cost(flops, nbytes):
    return pl.CostEstimate(flops=int(flops), bytes_accessed=int(nbytes), transcendentals=0)


def shards(state_field, spectral_weight, local_weight, channel_bias, cotangent):
    samples, yl = state_field.shape[:2]
    pencils = lax.axis_size("pencil")
    batches = lax.axis_size("batch")
    ml = spectral_weight.shape[0]
    mg = max(ml, 8)
    groups = MODES // mg
    deep = math.gcd(YB, yl)
    yblocks = yl // deep
    n = yl * C
    rows = 2 * ml
    mb = math.gcd(4, ml)

    ltf = jnp.asarray(z_forward_table())
    lti = jnp.asarray(z_inverse_table())
    xt = jnp.asarray(x_table())
    yf, yi = (jnp.asarray(t) for t in y_tables(yl))
    phase = jnp.asarray(phase_table(yl, pencils))
    sums = jnp.asarray(rows_table(rows))
    bias = channel_bias.reshape(1, C)

    def pack(v):
        if mg == ml:
            return v
        extra = v[:, 2 * mg :]
        v = v[:, : 2 * mg].reshape(groups, 2, mg // ml, ml, CQ)
        v = v.transpose(0, 2, 1, 3, 4).reshape(pencils, rows, CQ)
        extra = jnp.broadcast_to(extra[:1], (pencils,) + extra.shape[1:])
        return jnp.concatenate([v, extra], axis=1)

    def unpack(v):
        if mg == ml:
            return v
        v = v.reshape(groups, mg // ml, 2, ml, CQ).transpose(0, 2, 1, 3, 4)
        return v.reshape(groups, 2 * mg, CQ)

    def exchange(v):
        return lax.all_to_all(v, "pencil", 0, 0, tiled=True)

    def around(v):
        return [v] + [
            lax.ppermute(v, "batch", [(i, (i + k) % batches) for i in range(batches)])
            for k in range(1, batches)
        ]

    def cells(s):
        return pl.BlockSpec((1, deep, C, Z, X), lambda yb: (s, yb, 0, 0, 0))

    held = [pltpu.VMEM((yl, C, Z, X), F32), pltpu.SemaphoreType.DMA((yblocks,))]

    any_space = pl.BlockSpec(memory_space=pl.ANY)
    cell_bytes = 4 * yl * C * Z * X
    table_bytes = 2 * (yf.size + yi.size + xt.size)
    field = jax.ShapeDtypeStruct(state_field.shape, F32)
    one_field = jax.ShapeDtypeStruct((1,) + state_field.shape[1:], F32)
    x_spec, yf_spec, yi_spec = whole(xt.shape), whole(yf.shape), whole(yi.shape)
    ph_spec = whole(phase.shape)
    rk = pltpu.VMEM((n, ZJ * X), F32)
    qs = pltpu.VMEM((yl, 3 * ZJP * 8, GX), BF16)
    ws = pltpu.VMEM((512, 256), BF16)

    def forward(s):
        return pl.pallas_call(
            functools.partial(forward_kernel, s),
            grid=(yblocks,),
            in_specs=[any_space, whole(ltf.shape), x_spec, yf_spec, ph_spec],
            out_specs=whole((groups, 2 * mg, CQ)),
            out_shape=jax.ShapeDtypeStruct((groups, 2 * mg, CQ), F32),
            scratch_shapes=[rk] + held,
            compiler_params=params(),
            cost_estimate=cost(2e9, cell_bytes + table_bytes),
            name="forward",
        )(state_field, ltf, xt, yf, phase)

    def middle(s, modes, prev):
        aliases = {} if prev is None else {11: 0}
        more = [] if prev is None else [prev]
        return pl.pallas_call(
            functools.partial(cell_kernel, s),
            grid=(yblocks,),
            in_specs=[
                any_space, any_space, whole((groups, 2 * mg, CQ)), whole((C, C)),
                whole((1, C)), whole(ltf.shape), whole(lti.shape),
                x_spec, yf_spec, yi_spec, ph_spec,
            ] + [any_space] * len(more),
            out_specs=[cells(s), cells(0), whole((groups, 2 * mg + 8, CQ))],
            out_shape=[field, one_field, jax.ShapeDtypeStruct((groups, 2 * mg + 8, CQ), F32)],
            scratch_shapes=[
                rk, qs, ws, pltpu.VMEM((256, 256), F32), pltpu.VMEM((8, GX), F32),
            ] + held + held,
            input_output_aliases=aliases,
            compiler_params=params(),
            cost_estimate=cost(16e9, 4 * cell_bytes + table_bytes),
            name="middle",
        )(state_field, cotangent, modes, local_weight, bias, ltf, lti, xt, yf, yi, phase, *more)

    def backward(s, gp, modes, prev):
        aliases = {} if prev is None else {7: 0}
        more = [] if prev is None else [prev]
        return pl.pallas_call(
            back_kernel,
            grid=(yblocks,),
            in_specs=[
                any_space, whole((groups, 2 * mg, CQ)), whole((C, C)), whole(lti.shape),
                x_spec, yi_spec, ph_spec,
            ] + [any_space] * len(more),
            out_specs=cells(s),
            out_shape=field,
            scratch_shapes=[qs, ws] + held,
            input_output_aliases=aliases,
            compiler_params=params(),
            cost_estimate=cost(6e9, 2 * cell_bytes + table_bytes),
            name="backward",
        )(gp, modes, local_weight, lti, xt, yi, phase, *more)

    def turned(w):
        return pl.pallas_call(
            turn_kernel,
            grid=(ml // mb,),
            in_specs=[pl.BlockSpec((mb, 2, CQ, C), lambda m: (m, 0, 0, 0))],
            out_specs=pl.BlockSpec((mb, 2, C, CQ), lambda m: (m, 0, 0, 0)),
            out_shape=jax.ShapeDtypeStruct((ml, 2, C, CQ), F32),
            compiler_params=params(),
            cost_estimate=cost(0, 5 * 4 * ml * 2 * CQ * C),
            name="turn",
        )(w.transpose(0, 1, 2, 4, 3).reshape(ml, 2, CQ, C))

    def mix(kernel, v, wt, prev, name):
        shape = (pencils, rows, CQ)
        side = (v.shape[1] + (0 if prev is None else prev.shape[0]), CQ)
        args = [v, wt, sums] if prev is None else [v, wt, sums, prev]
        return pl.pallas_call(
            kernel,
            grid=(1,),
            in_specs=[whole(a.shape) for a in args],
            out_specs=[whole(shape), whole(side)],
            out_shape=[jax.ShapeDtypeStruct(shape, F32), jax.ShapeDtypeStruct(side, F32)],
            compiler_params=params(),
            cost_estimate=cost(2e8, 4 * (wt.size + 2 * v.size)),
            name=name,
        )(*args)

    def weight_gradient(sides, after):
        scaling = 1.0 / math.sqrt(samples * batches * X * Y * Z)
        gw, local, b = pl.pallas_call(
            lambda *refs: weight_kernel(scaling, samples, *refs),
            grid=(ml // mb,),
            in_specs=[whole(a.shape) for a in sides] + [any_space],
            out_specs=[
                pl.BlockSpec((mb, 2, CQ, C), lambda m: (m, 0, 0, 0)),
                whole((C, C)),
                whole((1, C)),
            ],
            out_shape=[
                jax.ShapeDtypeStruct((ml, 2, CQ, C), F32),
                jax.ShapeDtypeStruct((C, C), F32),
                jax.ShapeDtypeStruct((1, C), F32),
            ],
            scratch_shapes=[pltpu.VMEM((batches,) + sides[0].shape, F32)],
            compiler_params=params(),
            cost_estimate=cost(2e8, 4 * 4 * ml * 2 * CQ * C),
            name="weight",
        )(*sides, after)
        gw = gw.reshape(ml, 2, C, MY, C).transpose(0, 1, 2, 4, 3)
        return gw, local, b.reshape(C)

    every = range(samples)
    sent = [exchange(pack(forward(s))) for s in every]
    wt = turned(spectral_weight)
    modes, side = [], None
    for s in every:
        mixed, side = mix(mix_kernel, sent[s], wt, side, "mix")
        modes.append(unpack(exchange(mixed)))

    layer_out = None
    gps, backs = [], []
    for s in every:
        layer_out, gp, v = middle(s, modes[s], layer_out)
        gps.append(gp)
        b, side = mix(adjoint_kernel, exchange(pack(v)), wt, side, "adjoint")
        backs.append(unpack(exchange(b)))
    sides = around(side)
    grad_state = None
    for s in every:
        grad_state = backward(s, gps[s], backs[s], grad_state)
    gw, local, b = weight_gradient(sides, grad_state)
    return (layer_out, grad_state, gw, local, b)


def solution(mesh):
    return jax.shard_map(
        shards,
        mesh=mesh,
        in_specs=(
            P("batch", "pencil", None, None, None),
            P("pencil", None, None, None, None),
            P(),
            P(),
            P("batch", "pencil", None, None, None),
        ),
        out_specs=(
            P("batch", "pencil", None, None, None),
            P("batch", "pencil", None, None, None),
            P("pencil", None, None, None, None),
            P(),
            P(),
        ),
        check_vma=False,
    )
```

time: 1380 us -> 171 us (0.12)
  matrix products: 1030 us -> 0 us
  waiting for transfers between devices: 140 us -> 16.6 us
  Pallas kernels: 0 us -> 113 us
  local copies, waits for them, and re-layouts: 108 us -> 2.31 us
  blocking collectives: 41.1 us -> 0 us
  other arithmetic: 22.9 us -> 0 us
  starting transfers between devices: 16.9 us -> 37.4 us
  between operations: 14.8 us -> 0.84 us
    dot_general x55 -> x0, matrix products: 1030 us -> none  [contract(): return jnp.einsum(form, left, right, precision=lax.Precision.HIGHEST)]
    psum x1 -> x0, waiting for transfers between devices: 133 us -> none  [shards(): grad_spectral = lax.psum(weight_term(spectrum, grad_modes), 'batch')]
    pallas_call x0 -> x12, Pallas kernels: none -> 113 us  [the longest x2 47 us: middle(): pl.pallas_call(functools.partial(cell_kernel, s), grid=(yblocks,), in_spe...]
    unnamed x72 -> x22, local copies, waits for them, and re-layouts: 66.2 us -> 2.31 us
    psum x1 -> x0, blocking collectives: 41.1 us -> none  [shards(): lax.psum((local_term, bias_term), ('batch', 'pencil'))]
    all_to_all x7 -> x0, local copies, waits for them, and re-layouts: 16.7 us -> none  [the longest x4 10.5 us: from_spectrum(): lax.all_to_all(inverted, 'pencil', split_axis=4, concat_axis=0, tiled=True)]
    all_to_all x4 -> x8, starting transfers between devices: 16.9 us -> 31.8 us  [exchange(): return lax.all_to_all(v, 'pencil', 0, 0, tiled=True)]
  transfers between devices with their start and end apart: 5 -> 11, of which waited for: 2 -> 4; matrix products, arithmetic and copies ran while one was open for 18% -> 0% of each run, Pallas kernels for 0% -> 57%
where the time goes in v1:
time: 171 us; the launch traced here: 170 us
  Pallas kernels  113 us (66%)
  starting transfers between devices  37.4 us (22%)
  waiting for transfers between devices  16.6 us (10%)
  local copies, waits for them, and re-layouts  2.31 us (1%)
    pallas_call x2, Pallas kernels, middle(): pl.pallas_call(functools.partial(cell_kernel, s), grid=(yblocks,), in_spe...  47 us
    all_to_all x8, starting transfers between devices, exchange(): return lax.all_to_all(v, 'pencil', 0, 0, tiled=True)  31.8 us
    pallas_call x2, Pallas kernels, backward(): pl.pallas_call(back_kernel, grid=(yblocks,), in_specs=[any_space, whole((...  21.1 us
    all_to_all x8, waiting for transfers between devices, exchange(): return lax.all_to_all(v, 'pencil', 0, 0, tiled=True)  16.6 us
    pallas_call x2, Pallas kernels, forward(): pl.pallas_call(functools.partial(forward_kernel, s), grid=(yblocks,), in_...  15.7 us
    pallas_call x4, Pallas kernels, mix(): pl.pallas_call(kernel, grid=(1,), in_specs=[whole(a.shape) for a in args]...  13.8 us
    pallas_call x1, Pallas kernels, weight_gradient(): pl.pallas_call(lambda *refs: weight_kernel(scaling, samples, *refs), grid...  8.66 us
    pallas_call x1, Pallas kernels, turned(): pl.pallas_call(turn_kernel, grid=(ml // mb,), in_specs=[pl.BlockSpec((mb,...  6.35 us
  transfers between devices with their start and end apart: 11, of which 4 were waited for; matrix products, arithmetic and copies ran while one was open for 0% of the time, Pallas kernels for 57%

profile of v1, /device:TPU:0, one launch (start us, length us, event | category | flops | bytes accessed | tf_op | source)
XLA Modules:
  0.0 169.7 jit_solution(13017437168443813389)
XLA Ops:
  0.6 7.8 %forward.3 = f32[8,32,512]{2,1,0:T(8,128)} custom-call(f32[2,16,32,32,128]{4,3,2,1,0:T(8,128)} %x_ref.7, bf16[160,256]{1,0:T(8,128)(2,1)} %constant.14.clone.ltf_ref, bf16[512,1152]{1,0:T(8,128)(2,1)} %constant.16.clone.xt_ref, bf16[384,256]{1,0:T(8,128)(2,1)} %constant.17.clone.yf_ref, f32[8,8,512]{2,1,0:T(8,128)} %constant.19.clone.ph_ref), custom_call_target="tpu_custom_call" | custom-call | flops 2000000000 | bytes 9961472 | tf_op jit(solution)/shard_map/forward/pallas_call | solution.py:645
  8.5 5.2 %all-to-all-start.1 = ((f32[8,32,512]{2,1,0:T(8,128)}), f32[8,32,512]{2,1,0:T(8,128)S(1)}, u32[]{:S(2)}, u32[]{:S(2)}) async-start(f32[8,32,512]{2,1,0:T(8,128)} %forward.3), calls=%async_computation.1 | async-start | bytes 1048576 | tf_op jit(solution)/shard_map/all_to_all | solution.py:620
  13.7 7.8 %forward.2 = f32[8,32,512]{2,1,0:T(8,128)} custom-call(f32[2,16,32,32,128]{4,3,2,1,0:T(8,128)} %x_ref.7, bf16[160,256]{1,0:T(8,128)(2,1)} %constant.14.clone.ltf_ref, bf16[512,1152]{1,0:T(8,128)(2,1)} %constant.16.clone.xt_ref, bf16[384,256]{1,0:T(8,128)(2,1)} %constant.17.clone.yf_ref, f32[8,8,512]{2,1,0:T(8,128)} %constant.19.clone.ph_ref), custom_call_target="tpu_custom_call" | custom-call | flops 2000000000 | bytes 9961472 | tf_op jit(solution)/shard_map/forward/pallas_call | solution.py:645
  21.5 1.9 %all-to-all-done.1.v_ref = f32[8,32,512]{2,1,0:T(8,128)S(1)} async-done(((f32[8,32,512]{2,1,0:T(8,128)}), f32[8,32,512]{2,1,0:T(8,128)S(1)}, u32[]{:S(2)}, u32[]{:S(2)}) %all-to-all-start.1) | async-done | bytes 524320 | tf_op jit(solution)/shard_map/all_to_all | solution.py:620
  23.4 3.5 %all-to-all-start = ((f32[8,32,512]{2,1,0:T(8,128)}), f32[8,32,512]{2,1,0:T(8,128)S(1)}, u32[]{:S(2)}, u32[]{:S(2)}) async-start(f32[8,32,512]{2,1,0:T(8,128)} %forward.2), calls=%async_computation | async-start | bytes 1048576 | tf_op jit(solution)/shard_map/all_to_all | solution.py:620
  26.9 6.4 %turn.1.wt_ref = f32[16,2,32,512]{3,2,1,0:T(8,128)} custom-call(f32[16,2,512,32]{3,2,1,0:T(8,128)} %bitcast.8), custom_call_target="tpu_custom_call" | custom-call | bytes 10485760 | tf_op jit(solution)/shard_map/turn/pallas_call | solution.py:699
  33.3 0.0 copy-done.5
  33.3 3.4 %mix.2 = (f32[8,32,512]{2,1,0:T(8,128)}, f32[32,512]{1,0:T(8,128)}) custom-call(f32[8,32,512]{2,1,0:T(8,128)} %copy-done.5, f32[16,2,32,512]{3,2,1,0:T(8,128)} %turn.1.wt_ref, bf16[128,1024]{1,0:T(8,128)(2,1)} %constant.20.clone.sum_ref), custom_call_target="tpu_custom_call" | custom-call | flops 200000000 | bytes 3145728 | tf_op jit(solution)/shard_map/mix/pallas_call | solution.py:714
  36.7 0.0 all-to-all-done.v_ref
  36.7 4.1 %all-to-all-start.3 = ((f32[8,32,512]{2,1,0:T(8,128)}), f32[8,32,512]{2,1,0:T(8,128)S(1)}, u32[]{:S(2)}, u32[]{:S(2)}) async-start(f32[8,32,512]{2,1,0:T(8,128)} %get-tuple-element.24), calls=%async_computation.3 | async-start | bytes 1048576 | tf_op jit(solution)/shard_map/all_to_all | solution.py:620
  40.8 0.0 copy-done.4
  40.8 3.4 %mix.3 = (f32[8,32,512]{2,1,0:T(8,128)}, f32[64,512]{1,0:T(8,128)}) custom-call(f32[8,32,512]{2,1,0:T(8,128)} %copy-done.4, f32[16,2,32,512]{3,2,1,0:T(8,128)} %turn.1.wt_ref, bf16[128,1024]{1,0:T(8,128)(2,1)} %constant.20.clone.sum_ref, f32[32,512]{1,0:T(8,128)} %get-tuple-element.22.refs_0_), custom_call_target="tpu_custom_call" | custom-call | flops 200000000 | bytes 3145728 | tf_op jit(solution)/shard_map/mix/pallas_call | solution.py:714
  44.2 6.3 %all-to-all-done.3.m_ref = f32[8,32,512]{2,1,0:T(8,128)S(1)} async-done(((f32[8,32,512]{2,1,0:T(8,128)}), f32[8,32,512]{2,1,0:T(8,128)S(1)}, u32[]{:S(2)}, u32[]{:S(2)}) %all-to-all-start.3) | async-done | bytes 524320 | tf_op jit(solution)/shard_map/all_to_all | solution.py:620
  50.6 3.7 %all-to-all-start.2 = ((f32[8,32,512]{2,1,0:T(8,128)}), f32[8,32,512]{2,1,0:T(8,128)S(1)}, u32[]{:S(2)}, u32[]{:S(2)}) async-start(f32[8,32,512]{2,1,0:T(8,128)} %get-tuple-element.23), calls=%async_computation.2 | async-start | bytes 1048576 | tf_op jit(solution)/shard_map/all_to_all | solution.py:620
  54.2 0.0 copy-done.7
  54.3 23.5 %middle.2 = (f32[2,16,32,32,128]{4,3,2,1,0:T(8,128)}, f32[1,16,32,32,128]{4,3,2,1,0:T(8,128)}, f32[8,40,512]{2,1,0:T(8,128)}) custom-call(f32[2,16,32,32,128]{4,3,2,1,0:T(8,128)} %x_ref.7, f32[2,16,32,32,128]{4,3,2,1,0:T(8,128)} %ct_ref.3, f32[8,32,512]{2,1,0:T(8,128)} %copy-done.7, f32[32,32]{1,0:T(8,128)} %w_ref.7, f32[1,32]{1,0:T(1,128)} %bitcast.10, ...), custom_call_target="tpu_custom_call" | custom-call | flops 16000000000 | bytes 35127296 | tf_op jit(solution)/shard_map/middle/pallas_call | solution.py:660
  77.7 0.0 all-to-all-done.2.m_ref
  77.7 0.0 copy-start.6
  77.8 3.9 %all-to-all-start.5 = ((f32[8,40,512]{2,1,0:T(8,128)}), f32[8,40,512]{2,1,0:T(8,128)S(1)}, u32[]{:S(2)}, u32[]{:S(2)}) async-start(f32[8,40,512]{2,1,0:T(8,128)} %get-tuple-element.29), calls=%async_computation.5 | async-start | bytes 1310720 | tf_op jit(solution)/shard_map/all_to_all | solution.py:620
  81.7 0.0 copy-done.6
  81.7 23.5 %middle.3 = (f32[2,16,32,32,128]{4,3,2,1,0:T(8,128)}, f32[1,16,32,32,128]{4,3,2,1,0:T(8,128)}, f32[8,40,512]{2,1,0:T(8,128)}) custom-call(f32[2,16,32,32,128]{4,3,2,1,0:T(8,128)} %x_ref.7, f32[2,16,32,32,128]{4,3,2,1,0:T(8,128)} %ct_ref.3, f32[8,32,512]{2,1,0:T(8,128)} %copy-done.6, f32[32,32]{1,0:T(8,128)} %w_ref.7, ...), custom_call_target="tpu_custom_call", output_to_operand_aliasing={{0}: (11, {})} | custom-call | flops 16000000000 | bytes 35127296 | tf_op jit(solution)/shard_map/middle/pallas_call | solution.py:660
  105.2 0.0 all-to-all-done.5.v_ref
  105.2 0.0 copy-start
  105.2 4.2 %all-to-all-start.4 = ((f32[8,40,512]{2,1,0:T(8,128)}), f32[8,40,512]{2,1,0:T(8,128)S(1)}, u32[]{:S(2)}, u32[]{:S(2)}) async-start(f32[8,40,512]{2,1,0:T(8,128)} %get-tuple-element.28), calls=%async_computation.4 | async-start | bytes 1310720 | tf_op jit(solution)/shard_map/all_to_all | solution.py:620
  109.4 0.0 copy-done
  109.4 3.5 %adjoint.2 = (f32[8,32,512]{2,1,0:T(8,128)}, f32[104,512]{1,0:T(8,128)}) custom-call(f32[8,40,512]{2,1,0:T(8,128)} %copy-done, f32[16,2,32,512]{3,2,1,0:T(8,128)} %turn.1.wt_ref, bf16[128,1024]{1,0:T(8,128)(2,1)} %constant.20.clone.sum_ref, f32[64,512]{1,0:T(8,128)} %get-tuple-element.30.refs_0_), custom_call_target="tpu_custom_call" | custom-call | flops 200000000 | bytes 3407872 | tf_op jit(solution)/shard_map/adjoint/pallas_call | solution.py:714
  112.9 7.7 %all-to-all-done.4.v_ref = f32[8,40,512]{2,1,0:T(8,128)S(1)} async-done(((f32[8,40,512]{2,1,0:T(8,128)}), f32[8,40,512]{2,1,0:T(8,128)S(1)}, u32[]{:S(2)}, u32[]{:S(2)}) %all-to-all-start.4) | async-done | bytes 655392 | tf_op jit(solution)/shard_map/all_to_all | solution.py:620
  120.6 3.5 %all-to-all-start.7 = ((f32[8,32,512]{2,1,0:T(8,128)}), f32[8,32,512]{2,1,0:T(8,128)S(1)}, u32[]{:S(2)}, u32[]{:S(2)}) async-start(f32[8,32,512]{2,1,0:T(8,128)} %get-tuple-element.34), calls=%async_computation.7 | async-start | bytes 1048576 | tf_op jit(solution)/shard_map/all_to_all | solution.py:620
  124.1 0.0 copy-done.1
  124.1 3.5 %adjoint.3 = (f32[8,32,512]{2,1,0:T(8,128)}, f32[144,512]{1,0:T(8,128)}) custom-call(f32[8,40,512]{2,1,0:T(8,128)} %copy-done.1, f32[16,2,32,512]{3,2,1,0:T(8,128)} %turn.1.wt_ref, bf16[128,1024]{1,0:T(8,128)(2,1)} %constant.20.clone.sum_ref, f32[104,512]{1,0:T(8,128)} %get-tuple-element.31.refs_0_), custom_call_target="tpu_custom_call" | custom-call | flops 200000000 | bytes 3407872 | tf_op jit(solution)/shard_map/adjoint/pallas_call | solution.py:714
  127.6 1.6 collective-permute-start
  129.2 2.6 %collective-permute-start.1 = (f32[144,512]{1,0:T(8,128)}, f32[144,512]{1,0:T(8,128)S(1)}, u32[]{:S(2)}, u32[]{:S(2)}) collective-permute-start(f32[144,512]{1,0:T(8,128)} %get-tuple-element.35.refs_0_), channel_id=1, source_target_pairs={{0,16},{8,24},{16,0},{24,8},{1,17},{9,25},{17,1},{25,9},{2,18},{10... | collective-permute-start | bytes 884744 | tf_op jit(solution)/shard_map/ppermute | solution.py:624
  131.8 1.4 collective-permute-start.2
  133.1 0.6 all-to-all-done.7.m_ref
  133.8 3.8 %all-to-all-start.6 = ((f32[8,32,512]{2,1,0:T(8,128)}), f32[8,32,512]{2,1,0:T(8,128)S(1)}, u32[]{:S(2)}, u32[]{:S(2)}) async-start(f32[8,32,512]{2,1,0:T(8,128)} %get-tuple-element.32), calls=%async_computation.6 | async-start | bytes 1048576 | tf_op jit(solution)/shard_map/all_to_all | solution.py:620
  137.5 0.0 copy-done.3
  137.5 10.6 %backward.2.refs_0_ = f32[2,16,32,32,128]{4,3,2,1,0:T(8,128)} custom-call(f32[1,16,32,32,128]{4,3,2,1,0:T(8,128)} %get-tuple-element.33.gp_ref, f32[8,32,512]{2,1,0:T(8,128)} %copy-done.3, f32[32,32]{1,0:T(8,128)} %w_ref.7, bf16[256,240]{1,0:T(8,128)(2,1)} %constant.15.clone.lti_ref, bf16[512,1152]{1,0:T(8,128)(2,1)} %constant.16.clone.xt_ref, ...), custom_call_target="tpu_custom_call" | custom-call | flops 6000000000 | bytes 18350080 | tf_op jit(solution)/shard_map/backward/pallas_call | solution.py:682
  148.1 0.0 all-to-all-done.6.m_ref
  148.1 0.0 copy-start.2
  148.1 0.8 copy-done.2
  148.9 10.5 %backward.3.refs_4_ = f32[2,16,32,32,128]{4,3,2,1,0:T(8,128)} custom-call(f32[1,16,32,32,128]{4,3,2,1,0:T(8,128)} %get-tuple-element.27.gp_ref, f32[8,32,512]{2,1,0:T(8,128)} %copy-done.2, f32[32,32]{1,0:T(8,128)} %w_ref.7, bf16[256,240]{1,0:T(8,128)(2,1)} %constant.15.clone.lti_ref, ...), custom_call_target="tpu_custom_call", output_to_operand_aliasing={{}: (7, {})} | custom-call | flops 6000000000 | bytes 18350080 | tf_op jit(solution)/shard_map/backward/pallas_call | solution.py:682
  159.5 0.0 collective-permute-done.refs_1_
  159.5 0.0 collective-permute-done.1.refs_2_
  159.5 0.0 collective-permute-done.2.refs_3_
  159.5 0.7 copy-done.8
  160.2 0.1 copy-done.9
  160.3 0.7 copy-done.10
  161.0 8.7 %weight.1 = (f32[16,2,512,32]{3,2,1,0:T(8,128)}, f32[32,32]{1,0:T(8,128)}, f32[1,32]{1,0:T(1,128)}) custom-call(f32[144,512]{1,0:T(8,128)} %get-tuple-element.35.refs_0_, f32[144,512]{1,0:T(8,128)} %copy-done.8, f32[144,512]{1,0:T(8,128)} %copy-done.9, f32[144,512]{1,0:T(8,128)} %copy-done.10, f32[2,16,32,32,128]{4,3,2,1,0:T(8,128)} %backward.3.refs_4_), custom_call_target="tpu_custom_call" | custom-call | flops 200000000 | bytes 8388608 | tf_op jit(solution)/shard_map/weight/pallas_call | solution.py:727
  (8 shorter events, 0.0 us)
Async XLA Ops:
  8.5 14.9 %all-to-all-start.1 = ((f32[8,32,512]{2,1,0:T(8,128)}), f32[8,32,512]{2,1,0:T(8,128)S(1)}, u32[]{:S(2)}, u32[]{:S(2)}) async-start(f32[8,32,512]{2,1,0:T(8,128)} %forward.3), calls=%async_computation.1 | async-start | bytes 1048576 | tf_op jit(solution)/shard_map/all_to_all | solution.py:620
  23.4 9.9 %copy-start.5 = (f32[8,32,512]{2,1,0:T(8,128)}, f32[8,32,512]{2,1,0:T(8,128)S(1)}, u32[]{:S(2)}) copy-start(f32[8,32,512]{2,1,0:T(8,128)S(1)} %all-to-all-done.1.v_ref) | copy-start | bytes 1572868
  23.4 13.3 %all-to-all-start = ((f32[8,32,512]{2,1,0:T(8,128)}), f32[8,32,512]{2,1,0:T(8,128)S(1)}, u32[]{:S(2)}, u32[]{:S(2)}) async-start(f32[8,32,512]{2,1,0:T(8,128)} %forward.2), calls=%async_computation | async-start | bytes 1048576 | tf_op jit(solution)/shard_map/all_to_all | solution.py:620
  36.7 4.1 %copy-start.4 = (f32[8,32,512]{2,1,0:T(8,128)}, f32[8,32,512]{2,1,0:T(8,128)S(1)}, u32[]{:S(2)}) copy-start(f32[8,32,512]{2,1,0:T(8,128)S(1)} %all-to-all-done.v_ref) | copy-start | bytes 1572868
  36.7 13.9 %all-to-all-start.3 = ((f32[8,32,512]{2,1,0:T(8,128)}), f32[8,32,512]{2,1,0:T(8,128)S(1)}, u32[]{:S(2)}, u32[]{:S(2)}) async-start(f32[8,32,512]{2,1,0:T(8,128)} %get-tuple-element.24), calls=%async_computation.3 | async-start | bytes 1048576 | tf_op jit(solution)/shard_map/all_to_all | solution.py:620
  50.6 3.7 %copy-start.7 = (f32[8,32,512]{2,1,0:T(8,128)}, f32[8,32,512]{2,1,0:T(8,128)S(1)}, u32[]{:S(2)}) copy-start(f32[8,32,512]{2,1,0:T(8,128)S(1)} %all-to-all-done.3.m_ref) | copy-start | bytes 1572868
  50.6 27.2 %all-to-all-start.2 = ((f32[8,32,512]{2,1,0:T(8,128)}), f32[8,32,512]{2,1,0:T(8,128)S(1)}, u32[]{:S(2)}, u32[]{:S(2)}) async-start(f32[8,32,512]{2,1,0:T(8,128)} %get-tuple-element.23), calls=%async_computation.2 | async-start | bytes 1048576 | tf_op jit(solution)/shard_map/all_to_all | solution.py:620
  77.7 3.9 %copy-start.6 = (f32[8,32,512]{2,1,0:T(8,128)}, f32[8,32,512]{2,1,0:T(8,128)S(1)}, u32[]{:S(2)}) copy-start(f32[8,32,512]{2,1,0:T(8,128)S(1)} %all-to-all-done.2.m_ref) | copy-start | bytes 1572868
  77.8 27.5 %all-to-all-start.5 = ((f32[8,40,512]{2,1,0:T(8,128)}), f32[8,40,512]{2,1,0:T(8,128)S(1)}, u32[]{:S(2)}, u32[]{:S(2)}) async-start(f32[8,40,512]{2,1,0:T(8,128)} %get-tuple-element.29), calls=%async_computation.5 | async-start | bytes 1310720 | tf_op jit(solution)/shard_map/all_to_all | solution.py:620
  105.2 4.2 %copy-start = (f32[8,40,512]{2,1,0:T(8,128)}, f32[8,40,512]{2,1,0:T(8,128)S(1)}, u32[]{:S(2)}) copy-start(f32[8,40,512]{2,1,0:T(8,128)S(1)} %all-to-all-done.5.v_ref) | copy-start | bytes 1966084
  105.2 15.3 %all-to-all-start.4 = ((f32[8,40,512]{2,1,0:T(8,128)}), f32[8,40,512]{2,1,0:T(8,128)S(1)}, u32[]{:S(2)}, u32[]{:S(2)}) async-start(f32[8,40,512]{2,1,0:T(8,128)} %get-tuple-element.28), calls=%async_computation.4 | async-start | bytes 1310720 | tf_op jit(solution)/shard_map/all_to_all | solution.py:620
  120.6 3.5 %copy-start.1 = (f32[8,40,512]{2,1,0:T(8,128)}, f32[8,40,512]{2,1,0:T(8,128)S(1)}, u32[]{:S(2)}) copy-start(f32[8,40,512]{2,1,0:T(8,128)S(1)} %all-to-all-done.4.v_ref) | copy-start | bytes 1966084
  120.6 13.2 %all-to-all-start.7 = ((f32[8,32,512]{2,1,0:T(8,128)}), f32[8,32,512]{2,1,0:T(8,128)S(1)}, u32[]{:S(2)}, u32[]{:S(2)}) async-start(f32[8,32,512]{2,1,0:T(8,128)} %get-tuple-element.34), calls=%async_computation.7 | async-start | bytes 1048576 | tf_op jit(solution)/shard_map/all_to_all | solution.py:620
  127.6 31.9 %collective-permute-start = (f32[144,512]{1,0:T(8,128)}, f32[144,512]{1,0:T(8,128)S(1)}, u32[]{:S(2)}, u32[]{:S(2)}) collective-permute-start(f32[144,512]{1,0:T(8,128)} %get-tuple-element.35.refs_0_), channel_id=1, source_target_pairs={{0,8},{8,16},{16,24},{24,0},{1,9},{9,17},{17,25},{25,1},{2,10},{10... | collective-permute-start | bytes 884744 | tf_op jit(solution)/shard_map/ppermute | solution.py:624
  129.2 30.3 %collective-permute-start.1 = (f32[144,512]{1,0:T(8,128)}, f32[144,512]{1,0:T(8,128)S(1)}, u32[]{:S(2)}, u32[]{:S(2)}) collective-permute-start(f32[144,512]{1,0:T(8,128)} %get-tuple-element.35.refs_0_), channel_id=1, source_target_pairs={{0,16},{8,24},{16,0},{24,8},{1,17},{9,25},{17,1},{25,9},{2,18},{10... | collective-permute-start | bytes 884744 | tf_op jit(solution)/shard_map/ppermute | solution.py:624
  131.8 27.8 %collective-permute-start.2 = (f32[144,512]{1,0:T(8,128)}, f32[144,512]{1,0:T(8,128)S(1)}, u32[]{:S(2)}, u32[]{:S(2)}) collective-permute-start(f32[144,512]{1,0:T(8,128)} %get-tuple-element.35.refs_0_), channel_id=1, source_target_pairs={{0,24},{8,0},{16,8},{24,16},{1,25},{9,1},{17,9},{25,17},{2,26},{10... | collective-permute-start | bytes 884744 | tf_op jit(solution)/shard_map/ppermute | solution.py:624
  133.8 3.8 %copy-start.3 = (f32[8,32,512]{2,1,0:T(8,128)}, f32[8,32,512]{2,1,0:T(8,128)S(1)}, u32[]{:S(2)}) copy-start(f32[8,32,512]{2,1,0:T(8,128)S(1)} %all-to-all-done.7.m_ref) | copy-start | bytes 1572868
  133.8 14.4 %all-to-all-start.6 = ((f32[8,32,512]{2,1,0:T(8,128)}), f32[8,32,512]{2,1,0:T(8,128)S(1)}, u32[]{:S(2)}, u32[]{:S(2)}) async-start(f32[8,32,512]{2,1,0:T(8,128)} %get-tuple-element.32), calls=%async_computation.6 | async-start | bytes 1048576 | tf_op jit(solution)/shard_map/all_to_all | solution.py:620
  148.1 0.8 copy-start.2
  159.5 0.7 copy-start.8
  159.5 0.8 copy-start.9
  160.3 0.7 copy-start.10

commit v2 on v1

--- a/solution.py
+++ b/solution.py
@@ -22,7 +22,7 @@
 ZJ = 9
 ZJP = 10
 GX = 4 * X
-YB = 4
+YB = 2
 
 F32 = jnp.float32
 BF16 = jnp.bfloat16

time: 171 us -> 177 us (1.035)
  Pallas kernels: 113 us -> 119 us
    pallas_call x2, Pallas kernels: 47 us -> 50.9 us  [middle(): pl.pallas_call(functools.partial(cell_kernel, s), grid=(yblocks,), in_spe...]
    pallas_call x2, Pallas kernels: 21.1 us -> 23 us  [backward(): pl.pallas_call(back_kernel, grid=(yblocks,), in_specs=[any_space, whole((...]
  transfers between devices with their start and end apart: 11 -> 11, of which waited for: 4 -> 4; matrix products, arithmetic and copies ran while one was open for 0% -> 0% of each run, Pallas kernels for 57% -> 58%
where the time goes in v2:
time: 177 us; the launch traced here: 176 us
  Pallas kernels  119 us (67%)
  starting transfers between devices  37.4 us (21%)
  waiting for transfers between devices  16.2 us (9%)
  local copies, waits for them, and re-layouts  2.31 us (1%)
    pallas_call x2, Pallas kernels, middle(): pl.pallas_call(functools.partial(cell_kernel, s), grid=(yblocks,), in_spe...  50.9 us
    all_to_all x8, starting transfers between devices, exchange(): return lax.all_to_all(v, 'pencil', 0, 0, tiled=True)  31.8 us
    pallas_call x2, Pallas kernels, backward(): pl.pallas_call(back_kernel, grid=(yblocks,), in_specs=[any_space, whole((...  23 us
    pallas_call x2, Pallas kernels, forward(): pl.pallas_call(functools.partial(forward_kernel, s), grid=(yblocks,), in_...  16.4 us
    all_to_all x8, waiting for transfers between devices, exchange(): return lax.all_to_all(v, 'pencil', 0, 0, tiled=True)  16.2 us
    pallas_call x4, Pallas kernels, mix(): pl.pallas_call(kernel, grid=(1,), in_specs=[whole(a.shape) for a in args]...  13.8 us
    pallas_call x1, Pallas kernels, weight_gradient(): pl.pallas_call(lambda *refs: weight_kernel(scaling, samples, *refs), grid...  8.65 us
    pallas_call x1, Pallas kernels, turned(): pl.pallas_call(turn_kernel, grid=(ml // mb,), in_specs=[pl.BlockSpec((mb,...  6.35 us
  transfers between devices with their start and end apart: 11, of which 4 were waited for; matrix products, arithmetic and copies ran while one was open for 0% of the time, Pallas kernels for 58%

profile of v2, /device:TPU:0, one launch (start us, length us, event | category | flops | bytes accessed | tf_op | source)
XLA Modules:
  0.0 175.8 jit_solution(4062685416875535326)
XLA Ops:
  0.6 8.2 %forward.3 = f32[8,32,512]{2,1,0:T(8,128)} custom-call(f32[2,16,32,32,128]{4,3,2,1,0:T(8,128)} %x_ref.7, bf16[160,256]{1,0:T(8,128)(2,1)} %constant.14.clone.ltf_ref, bf16[512,1152]{1,0:T(8,128)(2,1)} %constant.16.clone.xt_ref, bf16[384,256]{1,0:T(8,128)(2,1)} %constant.17.clone.yf_ref, f32[8,8,512]{2,1,0:T(8,128)} %constant.19.clone.ph_ref), custom_call_target="tpu_custom_call" | custom-call | flops 2000000000 | bytes 9961472 | tf_op jit(solution)/shard_map/forward/pallas_call | solution.py:645
  8.8 5.2 %all-to-all-start.1 = ((f32[8,32,512]{2,1,0:T(8,128)}), f32[8,32,512]{2,1,0:T(8,128)S(1)}, u32[]{:S(2)}, u32[]{:S(2)}) async-start(f32[8,32,512]{2,1,0:T(8,128)} %forward.3), calls=%async_computation.1 | async-start | bytes 1048576 | tf_op jit(solution)/shard_map/all_to_all | solution.py:620
  14.0 8.2 %forward.2 = f32[8,32,512]{2,1,0:T(8,128)} custom-call(f32[2,16,32,32,128]{4,3,2,1,0:T(8,128)} %x_ref.7, bf16[160,256]{1,0:T(8,128)(2,1)} %constant.14.clone.ltf_ref, bf16[512,1152]{1,0:T(8,128)(2,1)} %constant.16.clone.xt_ref, bf16[384,256]{1,0:T(8,128)(2,1)} %constant.17.clone.yf_ref, f32[8,8,512]{2,1,0:T(8,128)} %constant.19.clone.ph_ref), custom_call_target="tpu_custom_call" | custom-call | flops 2000000000 | bytes 9961472 | tf_op jit(solution)/shard_map/forward/pallas_call | solution.py:645
  22.2 1.5 all-to-all-done.1.v_ref
  23.8 3.5 %all-to-all-start = ((f32[8,32,512]{2,1,0:T(8,128)}), f32[8,32,512]{2,1,0:T(8,128)S(1)}, u32[]{:S(2)}, u32[]{:S(2)}) async-start(f32[8,32,512]{2,1,0:T(8,128)} %forward.2), calls=%async_computation | async-start | bytes 1048576 | tf_op jit(solution)/shard_map/all_to_all | solution.py:620
  27.3 6.4 %turn.1.wt_ref = f32[16,2,32,512]{3,2,1,0:T(8,128)} custom-call(f32[16,2,512,32]{3,2,1,0:T(8,128)} %bitcast.8), custom_call_target="tpu_custom_call" | custom-call | bytes 10485760 | tf_op jit(solution)/shard_map/turn/pallas_call | solution.py:699
  33.6 0.0 copy-done.5
  33.6 3.4 %mix.2 = (f32[8,32,512]{2,1,0:T(8,128)}, f32[32,512]{1,0:T(8,128)}) custom-call(f32[8,32,512]{2,1,0:T(8,128)} %copy-done.5, f32[16,2,32,512]{3,2,1,0:T(8,128)} %turn.1.wt_ref, bf16[128,1024]{1,0:T(8,128)(2,1)} %constant.20.clone.sum_ref), custom_call_target="tpu_custom_call" | custom-call | flops 200000000 | bytes 3145728 | tf_op jit(solution)/shard_map/mix/pallas_call | solution.py:714
  37.0 0.0 all-to-all-done.v_ref
  37.1 4.1 %all-to-all-start.3 = ((f32[8,32,512]{2,1,0:T(8,128)}), f32[8,32,512]{2,1,0:T(8,128)S(1)}, u32[]{:S(2)}, u32[]{:S(2)}) async-start(f32[8,32,512]{2,1,0:T(8,128)} %get-tuple-element.24), calls=%async_computation.3 | async-start | bytes 1048576 | tf_op jit(solution)/shard_map/all_to_all | solution.py:620
  41.2 0.0 copy-done.4
  41.2 3.4 %mix.3 = (f32[8,32,512]{2,1,0:T(8,128)}, f32[64,512]{1,0:T(8,128)}) custom-call(f32[8,32,512]{2,1,0:T(8,128)} %copy-done.4, f32[16,2,32,512]{3,2,1,0:T(8,128)} %turn.1.wt_ref, bf16[128,1024]{1,0:T(8,128)(2,1)} %constant.20.clone.sum_ref, f32[32,512]{1,0:T(8,128)} %get-tuple-element.22.refs_0_), custom_call_target="tpu_custom_call" | custom-call | flops 200000000 | bytes 3145728 | tf_op jit(solution)/shard_map/mix/pallas_call | solution.py:714
  44.6 6.3 %all-to-all-done.3.m_ref = f32[8,32,512]{2,1,0:T(8,128)S(1)} async-done(((f32[8,32,512]{2,1,0:T(8,128)}), f32[8,32,512]{2,1,0:T(8,128)S(1)}, u32[]{:S(2)}, u32[]{:S(2)}) %all-to-all-start.3) | async-done | bytes 524320 | tf_op jit(solution)/shard_map/all_to_all | solution.py:620
  50.9 3.5 %all-to-all-start.2 = ((f32[8,32,512]{2,1,0:T(8,128)}), f32[8,32,512]{2,1,0:T(8,128)S(1)}, u32[]{:S(2)}, u32[]{:S(2)}) async-start(f32[8,32,512]{2,1,0:T(8,128)} %get-tuple-element.23), calls=%async_computation.2 | async-start | bytes 1048576 | tf_op jit(solution)/shard_map/all_to_all | solution.py:620
  54.4 0.0 copy-done.7
  54.4 25.4 %middle.2 = (f32[2,16,32,32,128]{4,3,2,1,0:T(8,128)}, f32[1,16,32,32,128]{4,3,2,1,0:T(8,128)}, f32[8,40,512]{2,1,0:T(8,128)}) custom-call(f32[2,16,32,32,128]{4,3,2,1,0:T(8,128)} %x_ref.7, f32[2,16,32,32,128]{4,3,2,1,0:T(8,128)} %ct_ref.3, f32[8,32,512]{2,1,0:T(8,128)} %copy-done.7, f32[32,32]{1,0:T(8,128)} %w_ref.7, f32[1,32]{1,0:T(1,128)} %bitcast.10, ...), custom_call_target="tpu_custom_call" | custom-call | flops 16000000000 | bytes 35127296 | tf_op jit(solution)/shard_map/middle/pallas_call | solution.py:660
  79.8 0.0 all-to-all-done.2.m_ref
  79.9 0.0 copy-start.6
  79.9 4.1 %all-to-all-start.5 = ((f32[8,40,512]{2,1,0:T(8,128)}), f32[8,40,512]{2,1,0:T(8,128)S(1)}, u32[]{:S(2)}, u32[]{:S(2)}) async-start(f32[8,40,512]{2,1,0:T(8,128)} %get-tuple-element.29), calls=%async_computation.5 | async-start | bytes 1310720 | tf_op jit(solution)/shard_map/all_to_all | solution.py:620
  84.0 0.0 copy-done.6
  84.0 25.5 %middle.3 = (f32[2,16,32,32,128]{4,3,2,1,0:T(8,128)}, f32[1,16,32,32,128]{4,3,2,1,0:T(8,128)}, f32[8,40,512]{2,1,0:T(8,128)}) custom-call(f32[2,16,32,32,128]{4,3,2,1,0:T(8,128)} %x_ref.7, f32[2,16,32,32,128]{4,3,2,1,0:T(8,128)} %ct_ref.3, f32[8,32,512]{2,1,0:T(8,128)} %copy-done.6, f32[32,32]{1,0:T(8,128)} %w_ref.7, ...), custom_call_target="tpu_custom_call", output_to_operand_aliasing={{0}: (11, {})} | custom-call | flops 16000000000 | bytes 35127296 | tf_op jit(solution)/shard_map/middle/pallas_call | solution.py:660
  109.5 0.0 all-to-all-done.5.v_ref
  109.5 0.0 copy-start
  109.5 4.2 %all-to-all-start.4 = ((f32[8,40,512]{2,1,0:T(8,128)}), f32[8,40,512]{2,1,0:T(8,128)S(1)}, u32[]{:S(2)}, u32[]{:S(2)}) async-start(f32[8,40,512]{2,1,0:T(8,128)} %get-tuple-element.28), calls=%async_computation.4 | async-start | bytes 1310720 | tf_op jit(solution)/shard_map/all_to_all | solution.py:620
  113.7 0.0 copy-done
  113.7 3.4 %adjoint.2 = (f32[8,32,512]{2,1,0:T(8,128)}, f32[104,512]{1,0:T(8,128)}) custom-call(f32[8,40,512]{2,1,0:T(8,128)} %copy-done, f32[16,2,32,512]{3,2,1,0:T(8,128)} %turn.1.wt_ref, bf16[128,1024]{1,0:T(8,128)(2,1)} %constant.20.clone.sum_ref, f32[64,512]{1,0:T(8,128)} %get-tuple-element.30.refs_0_), custom_call_target="tpu_custom_call" | custom-call | flops 200000000 | bytes 3407872 | tf_op jit(solution)/shard_map/adjoint/pallas_call | solution.py:714
  117.1 7.7 %all-to-all-done.4.v_ref = f32[8,40,512]{2,1,0:T(8,128)S(1)} async-done(((f32[8,40,512]{2,1,0:T(8,128)}), f32[8,40,512]{2,1,0:T(8,128)S(1)}, u32[]{:S(2)}, u32[]{:S(2)}) %all-to-all-start.4) | async-done | bytes 655392 | tf_op jit(solution)/shard_map/all_to_all | solution.py:620
  124.8 3.5 %all-to-all-start.7 = ((f32[8,32,512]{2,1,0:T(8,128)}), f32[8,32,512]{2,1,0:T(8,128)S(1)}, u32[]{:S(2)}, u32[]{:S(2)}) async-start(f32[8,32,512]{2,1,0:T(8,128)} %get-tuple-element.34), calls=%async_computation.7 | async-start | bytes 1048576 | tf_op jit(solution)/shard_map/all_to_all | solution.py:620
  128.3 0.0 copy-done.1
  128.3 3.5 %adjoint.3 = (f32[8,32,512]{2,1,0:T(8,128)}, f32[144,512]{1,0:T(8,128)}) custom-call(f32[8,40,512]{2,1,0:T(8,128)} %copy-done.1, f32[16,2,32,512]{3,2,1,0:T(8,128)} %turn.1.wt_ref, bf16[128,1024]{1,0:T(8,128)(2,1)} %constant.20.clone.sum_ref, f32[104,512]{1,0:T(8,128)} %get-tuple-element.31.refs_0_), custom_call_target="tpu_custom_call" | custom-call | flops 200000000 | bytes 3407872 | tf_op jit(solution)/shard_map/adjoint/pallas_call | solution.py:714
  131.8 1.6 collective-permute-start
  133.4 2.6 %collective-permute-start.1 = (f32[144,512]{1,0:T(8,128)}, f32[144,512]{1,0:T(8,128)S(1)}, u32[]{:S(2)}, u32[]{:S(2)}) collective-permute-start(f32[144,512]{1,0:T(8,128)} %get-tuple-element.35.refs_0_), channel_id=1, source_target_pairs={{0,16},{8,24},{16,0},{24,8},{1,17},{9,25},{17,1},{25,9},{2,18},{10... | collective-permute-start | bytes 884744 | tf_op jit(solution)/shard_map/ppermute | solution.py:624
  136.0 1.3 collective-permute-start.2
  137.4 0.7 all-to-all-done.7.m_ref
  138.0 3.7 %all-to-all-start.6 = ((f32[8,32,512]{2,1,0:T(8,128)}), f32[8,32,512]{2,1,0:T(8,128)S(1)}, u32[]{:S(2)}, u32[]{:S(2)}) async-start(f32[8,32,512]{2,1,0:T(8,128)} %get-tuple-element.32), calls=%async_computation.6 | async-start | bytes 1048576 | tf_op jit(solution)/shard_map/all_to_all | solution.py:620
  141.7 11.5 %backward.2.refs_0_ = f32[2,16,32,32,128]{4,3,2,1,0:T(8,128)} custom-call(f32[1,16,32,32,128]{4,3,2,1,0:T(8,128)} %get-tuple-element.33.gp_ref, f32[8,32,512]{2,1,0:T(8,128)} %copy-done.3, f32[32,32]{1,0:T(8,128)} %w_ref.7, bf16[256,240]{1,0:T(8,128)(2,1)} %constant.15.clone.lti_ref, bf16[512,1152]{1,0:T(8,128)(2,1)} %constant.16.clone.xt_ref, ...), custom_call_target="tpu_custom_call" | custom-call | flops 6000000000 | bytes 18350080 | tf_op jit(solution)/shard_map/backward/pallas_call | solution.py:682
  153.3 0.0 all-to-all-done.6.m_ref
  153.3 0.0 copy-start.2
  153.3 0.8 copy-done.2
  154.1 11.5 %backward.3.refs_4_ = f32[2,16,32,32,128]{4,3,2,1,0:T(8,128)} custom-call(f32[1,16,32,32,128]{4,3,2,1,0:T(8,128)} %get-tuple-element.27.gp_ref, f32[8,32,512]{2,1,0:T(8,128)} %copy-done.2, f32[32,32]{1,0:T(8,128)} %w_ref.7, bf16[256,240]{1,0:T(8,128)(2,1)} %constant.15.clone.lti_ref, ...), custom_call_target="tpu_custom_call", output_to_operand_aliasing={{}: (7, {})} | custom-call | flops 6000000000 | bytes 18350080 | tf_op jit(solution)/shard_map/backward/pallas_call | solution.py:682
  165.6 0.0 collective-permute-done.refs_1_
  165.6 0.0 collective-permute-done.1.refs_2_
  165.6 0.0 copy-start.9
  165.6 0.0 collective-permute-done.2.refs_3_
  165.6 0.7 copy-done.8
  166.3 0.1 copy-done.9
  166.4 0.7 copy-done.10
  167.1 8.6 %weight.1 = (f32[16,2,512,32]{3,2,1,0:T(8,128)}, f32[32,32]{1,0:T(8,128)}, f32[1,32]{1,0:T(1,128)}) custom-call(f32[144,512]{1,0:T(8,128)} %get-tuple-element.35.refs_0_, f32[144,512]{1,0:T(8,128)} %copy-done.8, f32[144,512]{1,0:T(8,128)} %copy-done.9, f32[144,512]{1,0:T(8,128)} %copy-done.10, f32[2,16,32,32,128]{4,3,2,1,0:T(8,128)} %backward.3.refs_4_), custom_call_target="tpu_custom_call" | custom-call | flops 200000000 | bytes 8388608 | tf_op jit(solution)/shard_map/weight/pallas_call | solution.py:727
  (8 shorter events, 0.0 us)
Async XLA Ops:
  8.8 14.9 %all-to-all-start.1 = ((f32[8,32,512]{2,1,0:T(8,128)}), f32[8,32,512]{2,1,0:T(8,128)S(1)}, u32[]{:S(2)}, u32[]{:S(2)}) async-start(f32[8,32,512]{2,1,0:T(8,128)} %forward.3), calls=%async_computation.1 | async-start | bytes 1048576 | tf_op jit(solution)/shard_map/all_to_all | solution.py:620
  23.8 9.9 %copy-start.5 = (f32[8,32,512]{2,1,0:T(8,128)}, f32[8,32,512]{2,1,0:T(8,128)S(1)}, u32[]{:S(2)}) copy-start(f32[8,32,512]{2,1,0:T(8,128)S(1)} %all-to-all-done.1.v_ref) | copy-start | bytes 1572868
  23.8 13.3 %all-to-all-start = ((f32[8,32,512]{2,1,0:T(8,128)}), f32[8,32,512]{2,1,0:T(8,128)S(1)}, u32[]{:S(2)}, u32[]{:S(2)}) async-start(f32[8,32,512]{2,1,0:T(8,128)} %forward.2), calls=%async_computation | async-start | bytes 1048576 | tf_op jit(solution)/shard_map/all_to_all | solution.py:620
  37.1 4.1 %copy-start.4 = (f32[8,32,512]{2,1,0:T(8,128)}, f32[8,32,512]{2,1,0:T(8,128)S(1)}, u32[]{:S(2)}) copy-start(f32[8,32,512]{2,1,0:T(8,128)S(1)} %all-to-all-done.v_ref) | copy-start | bytes 1572868
  37.1 13.9 %all-to-all-start.3 = ((f32[8,32,512]{2,1,0:T(8,128)}), f32[8,32,512]{2,1,0:T(8,128)S(1)}, u32[]{:S(2)}, u32[]{:S(2)}) async-start(f32[8,32,512]{2,1,0:T(8,128)} %get-tuple-element.24), calls=%async_computation.3 | async-start | bytes 1048576 | tf_op jit(solution)/shard_map/all_to_all | solution.py:620
  50.9 3.5 %copy-start.7 = (f32[8,32,512]{2,1,0:T(8,128)}, f32[8,32,512]{2,1,0:T(8,128)S(1)}, u32[]{:S(2)}) copy-start(f32[8,32,512]{2,1,0:T(8,128)S(1)} %all-to-all-done.3.m_ref) | copy-start | bytes 1572868
  50.9 28.9 %all-to-all-start.2 = ((f32[8,32,512]{2,1,0:T(8,128)}), f32[8,32,512]{2,1,0:T(8,128)S(1)}, u32[]{:S(2)}, u32[]{:S(2)}) async-start(f32[8,32,512]{2,1,0:T(8,128)} %get-tuple-element.23), calls=%async_computation.2 | async-start | bytes 1048576 | tf_op jit(solution)/shard_map/all_to_all | solution.py:620
  79.9 4.1 %copy-start.6 = (f32[8,32,512]{2,1,0:T(8,128)}, f32[8,32,512]{2,1,0:T(8,128)S(1)}, u32[]{:S(2)}) copy-start(f32[8,32,512]{2,1,0:T(8,128)S(1)} %all-to-all-done.2.m_ref) | copy-start | bytes 1572868
  79.9 29.6 %all-to-all-start.5 = ((f32[8,40,512]{2,1,0:T(8,128)}), f32[8,40,512]{2,1,0:T(8,128)S(1)}, u32[]{:S(2)}, u32[]{:S(2)}) async-start(f32[8,40,512]{2,1,0:T(8,128)} %get-tuple-element.29), calls=%async_computation.5 | async-start | bytes 1310720 | tf_op jit(solution)/shard_map/all_to_all | solution.py:620
  109.5 4.2 %copy-start = (f32[8,40,512]{2,1,0:T(8,128)}, f32[8,40,512]{2,1,0:T(8,128)S(1)}, u32[]{:S(2)}) copy-start(f32[8,40,512]{2,1,0:T(8,128)S(1)} %all-to-all-done.5.v_ref) | copy-start | bytes 1966084
  109.5 15.4 %all-to-all-start.4 = ((f32[8,40,512]{2,1,0:T(8,128)}), f32[8,40,512]{2,1,0:T(8,128)S(1)}, u32[]{:S(2)}, u32[]{:S(2)}) async-start(f32[8,40,512]{2,1,0:T(8,128)} %get-tuple-element.28), calls=%async_computation.4 | async-start | bytes 1310720 | tf_op jit(solution)/shard_map/all_to_all | solution.py:620
  124.8 3.5 %copy-start.1 = (f32[8,40,512]{2,1,0:T(8,128)}, f32[8,40,512]{2,1,0:T(8,128)S(1)}, u32[]{:S(2)}) copy-start(f32[8,40,512]{2,1,0:T(8,128)S(1)} %all-to-all-done.4.v_ref) | copy-start | bytes 1966084
  124.8 13.2 %all-to-all-start.7 = ((f32[8,32,512]{2,1,0:T(8,128)}), f32[8,32,512]{2,1,0:T(8,128)S(1)}, u32[]{:S(2)}, u32[]{:S(2)}) async-start(f32[8,32,512]{2,1,0:T(8,128)} %get-tuple-element.34), calls=%async_computation.7 | async-start | bytes 1048576 | tf_op jit(solution)/shard_map/all_to_all | solution.py:620
  131.8 33.8 %collective-permute-start = (f32[144,512]{1,0:T(8,128)}, f32[144,512]{1,0:T(8,128)S(1)}, u32[]{:S(2)}, u32[]{:S(2)}) collective-permute-start(f32[144,512]{1,0:T(8,128)} %get-tuple-element.35.refs_0_), channel_id=1, source_target_pairs={{0,8},{8,16},{16,24},{24,0},{1,9},{9,17},{17,25},{25,1},{2,10},{10... | collective-permute-start | bytes 884744 | tf_op jit(solution)/shard_map/ppermute | solution.py:624
  133.4 32.2 %collective-permute-start.1 = (f32[144,512]{1,0:T(8,128)}, f32[144,512]{1,0:T(8,128)S(1)}, u32[]{:S(2)}, u32[]{:S(2)}) collective-permute-start(f32[144,512]{1,0:T(8,128)} %get-tuple-element.35.refs_0_), channel_id=1, source_target_pairs={{0,16},{8,24},{16,0},{24,8},{1,17},{9,25},{17,1},{25,9},{2,18},{10... | collective-permute-start | bytes 884744 | tf_op jit(solution)/shard_map/ppermute | solution.py:624
  136.0 29.6 %collective-permute-start.2 = (f32[144,512]{1,0:T(8,128)}, f32[144,512]{1,0:T(8,128)S(1)}, u32[]{:S(2)}, u32[]{:S(2)}) collective-permute-start(f32[144,512]{1,0:T(8,128)} %get-tuple-element.35.refs_0_), channel_id=1, source_target_pairs={{0,24},{8,0},{16,8},{24,16},{1,25},{9,1},{17,9},{25,17},{2,26},{10... | collective-permute-start | bytes 884744 | tf_op jit(solution)/shard_map/ppermute | solution.py:624
  138.0 3.7 %copy-start.3 = (f32[8,32,512]{2,1,0:T(8,128)}, f32[8,32,512]{2,1,0:T(8,128)S(1)}, u32[]{:S(2)}) copy-start(f32[8,32,512]{2,1,0:T(8,128)S(1)} %all-to-all-done.7.m_ref) | copy-start | bytes 1572868
  138.0 15.3 %all-to-all-start.6 = ((f32[8,32,512]{2,1,0:T(8,128)}), f32[8,32,512]{2,1,0:T(8,128)S(1)}, u32[]{:S(2)}, u32[]{:S(2)}) async-start(f32[8,32,512]{2,1,0:T(8,128)} %get-tuple-element.32), calls=%async_computation.6 | async-start | bytes 1048576 | tf_op jit(solution)/shard_map/all_to_all | solution.py:620
  153.3 0.8 copy-start.2
  165.6 0.7 copy-start.8
  165.6 0.8 copy-start.9
  166.4 0.7 copy-start.10
